TPU v7x, 256 devices: a whole 4x4x8 slice. The times are simulated.
256 devices in a mesh: tm: 64 (over z, y, core), head: 4 (over x).
Axes of the slice: x: 4, y: 4, z: 8, core: 2. Of those that a mesh axis runs over, the one named last changes fastest.
Arguments:
- video_qkv: bfloat16 [3, 32768, 3072], P(None, 'tm', 'head'), may hold values from -1600 to 1600
- audio_qkv: bfloat16 [3, 64, 256, 3072], P(None, None, 'tm', 'head'), may hold values from -1600 to 1600
- video_gain: float32 [2, 3072], P(None, 'head'), may hold values from 1 to 2
- audio_gain: float32 [2, 3072], P(None, 'head'), may hold values from 1 to 2
- video_cot: bfloat16 [32768, 3072], P('tm', 'head'), may hold values from -6 to 6
- audio_cot: bfloat16 [64, 256, 3072], P(None, 'tm', 'head'), may hold values from -6 to 6
- intersection: int32 [4096, 2], replicated, may hold values from 0 to 255, as said below
- lengths: int32 [4096], replicated, may hold values from 1 to 4, as said below
Outputs:
- out_video: bfloat16 [32768, 3072], P('tm', 'head')
- out_audio: bfloat16 [64, 256, 3072], P(None, 'tm', 'head')
- grad_video: bfloat16 [3, 32768, 3072], P(None, 'tm', 'head')
- grad_audio: bfloat16 [3, 64, 256, 3072], P(None, None, 'tm', 'head')
Inputs may be any that keep to these rules, and one draw needn't show every extreme that they name: With c = g * 4 // 64, intersection[g, 0] is c or c - 1 and intersection[g, 1] is c or c + 1, both within the clip's video blocks. `lengths`: some blocks are full.
All inputs are finite; a program needn't handle non-finite values.
Results may differ from a plain program's by a relative error of at most 0.007.
The roundings to bfloat16 on the way count: a program that leaves them out, or rounds other values in their place, can miss the bound.
Values may be sent and summed in bfloat16 or wider, within the bound.
A program may use at most 128 MiB of HBM per device.

v0:
```python
import jax
import jax.numpy as jnp
from jax import lax
from jax.sharding import PartitionSpec as P

HEADS = 24
HD = 128
VB = 4
VBLK = 128


EPSILON = 1e-06
NEGATIVE = -1e30


def padded_2(x, sides, width):
    for axis, dim in sides:
        size, length = (lax.axis_size(axis), x.shape[dim])
        up = [(i, (i + 1) % size) for i in range(size - 1)]
        down = [(j, i) for i, j in up]
        last = lax.slice_in_dim(x, length - width, length, axis=dim)
        first = lax.slice_in_dim(x, 0, width, axis=dim)
        before = lax.ppermute(last, axis, up)
        after = lax.ppermute(first, axis, down)
        x = jnp.concatenate([before, x, after], axis=dim)
    return x


def attend(queries, keyset, values, paired, cotangent):
    softmax_scale = queries.shape[-1] ** (-0.5)
    scores = (
        jnp.einsum("qhe,khe->hqk", queries, keyset, preferred_element_type=jnp.float32)
        * softmax_scale
    )
    scores = jnp.where(paired[None], scores, NEGATIVE)
    row_max = jnp.max(scores, -1, keepdims=True)
    exponent = jnp.exp(scores - row_max)
    attention = (exponent / jnp.sum(exponent, -1, keepdims=True)).astype(jnp.bfloat16)
    output = jnp.einsum("hqk,khe->qhe", attention, values, preferred_element_type=jnp.float32)
    value_grad = jnp.einsum(
        "hqk,qhe->khe", attention, cotangent, preferred_element_type=jnp.float32
    )
    prob_grad = jnp.einsum("qhe,khe->hqk", cotangent, values, preferred_element_type=jnp.float32)
    widened = lax.optimization_barrier(attention).astype(jnp.float32)
    score_grad = (widened * (prob_grad - jnp.sum(prob_grad * widened, -1, keepdims=True))).astype(
        jnp.bfloat16
    )
    query_grad = (
        jnp.einsum("hqk,khe->qhe", score_grad, keyset, preferred_element_type=jnp.float32)
        * softmax_scale
    )
    key_grad = (
        jnp.einsum("hqk,qhe->khe", score_grad, queries, preferred_element_type=jnp.float32)
        * softmax_scale
    )
    return (output, query_grad, key_grad, value_grad)


def to_heads(array):
    return array.reshape(array.shape[0], -1, HD)


def to_rows(array):
    return array.reshape(array.shape[0], -1)


def cross_window(
    position,
    video_query,
    video_pairs,
    video_cotangent,
    audio_query,
    audio_pairs,
    audio_cotangent,
    low_table,
    high_table,
    live_table,
    sub_blocks,
    video_block,
    audio_block,
    edge_blocks,
):
    video_rows = video_query.shape[0]
    audio_rows = audio_query.shape[0]
    video_sub = position * sub_blocks + jnp.arange(video_rows, dtype=jnp.int32) // video_block
    key_low = jnp.repeat(low_table, audio_block)
    key_high = jnp.repeat(high_table, audio_block)
    key_live = jnp.arange(key_low.shape[0], dtype=jnp.int32) % audio_block < jnp.repeat(
        live_table, audio_block
    )
    paired_va = (
        (key_low[None] <= video_sub[:, None])
        & (video_sub[:, None] <= key_high[None])
        & key_live[None]
    )
    start = edge_blocks * audio_block
    query_low = key_low[start : start + audio_rows]
    query_high = key_high[start : start + audio_rows]
    query_live = key_live[start : start + audio_rows]
    key_sub = (
        position * sub_blocks - 1 + jnp.arange(video_pairs.shape[1], dtype=jnp.int32) // video_block
    )
    paired_av = (query_low[:, None] <= key_sub[None]) & (key_sub[None] <= query_high[:, None])
    cot_live = jnp.where(query_live[:, None], audio_cotangent, jnp.zeros_like(audio_cotangent))
    out_va, dq_video, dk_audio, dv_audio = attend(
        to_heads(video_query),
        to_heads(audio_pairs[0]),
        to_heads(audio_pairs[1]),
        paired_va,
        to_heads(video_cotangent),
    )
    out_av, dq_audio, dk_video, dv_video = attend(
        to_heads(audio_query),
        to_heads(video_pairs[0]),
        to_heads(video_pairs[1]),
        paired_av,
        to_heads(cot_live),
    )
    audio_out = to_rows(out_av).astype(jnp.bfloat16)
    audio_out = jnp.where(query_live[:, None], audio_out, jnp.zeros_like(audio_out))
    return (
        to_rows(out_va).astype(jnp.bfloat16),
        audio_out,
        to_rows(dq_video),
        jnp.stack([to_rows(dk_video), to_rows(dv_video)]),
        to_rows(dq_audio),
        jnp.stack([to_rows(dk_audio), to_rows(dv_audio)]),
    )


def settle(extended, arrived, margin):
    center = extended[:, margin : extended.shape[1] - margin]
    row_count = center.shape[1]
    total = center + jnp.pad(arrived[:, :margin], ((0, 0), (0, row_count - margin), (0, 0)))
    return total + jnp.pad(
        arrived[:, arrived.shape[1] - margin :], ((0, 0), (row_count - margin, 0), (0, 0))
    )


def square_sums(array):
    widened = array.astype(jnp.float32)
    return jnp.sum(widened * widened, -1)


def window_table(column, filler, position, owners, edge_blocks):
    padded = jnp.pad(column, (edge_blocks, edge_blocks), constant_values=filler)
    return lax.dynamic_slice_in_dim(padded, position * owners, owners + 2 * edge_blocks, 0)


def local(
    video_qkv, audio_qkv, video_gain, audio_gain, video_cot, audio_cot, intersection, lengths
):
    owners = lax.axis_size("tm")
    position = lax.axis_index("tm")
    audio_block = audio_qkv.shape[2]
    edge_blocks = owners // VB
    edge_rows = edge_blocks * audio_block
    feat_all = HEADS * HD
    squares = lax.psum((square_sums(video_qkv[:2]), square_sums(audio_qkv[:2])), "head")
    video_rate = lax.rsqrt(squares[0] / feat_all + EPSILON)
    audio_rate = lax.rsqrt(squares[1] / feat_all + EPSILON)
    video_normed = (
        video_qkv[:2].astype(jnp.float32) * video_rate[..., None] * video_gain[:, None, :]
    ).astype(jnp.bfloat16)
    audio_normed = (
        audio_qkv[:2].astype(jnp.float32) * audio_rate[..., None] * audio_gain[:, None, None, :]
    ).astype(jnp.bfloat16)
    outgoing = jnp.concatenate([audio_normed, audio_qkv[2:], audio_cot[None]], 0)
    arrived = lax.all_to_all(outgoing, "tm", split_axis=1, concat_axis=1, tiled=True)
    aligned = arrived.reshape(4, owners * audio_block, -1)
    audio_pairs = padded_2(aligned[1:3], (("tm", 1),), edge_rows)
    video_pairs = padded_2(jnp.stack([video_normed[1], video_qkv[2]]), (("tm", 1),), VBLK)
    low_table = window_table(intersection[:, 0], 1073741824, position, owners, edge_blocks)
    high_table = window_table(intersection[:, 1], -1, position, owners, edge_blocks)
    live_table = window_table(lengths, 0, position, owners, edge_blocks)
    results = cross_window(
        position,
        video_normed[0],
        video_pairs,
        video_cot,
        aligned[0],
        audio_pairs,
        aligned[3],
        low_table,
        high_table,
        live_table,
        VB,
        VBLK,
        audio_block,
        edge_blocks,
    )
    out_video, audio_out, video_q_grad, video_kv_ext, audio_q_grad, audio_kv_ext = results
    video_edge = jnp.concatenate(
        [video_kv_ext[:, :VBLK], video_kv_ext[:, video_kv_ext.shape[1] - VBLK :]], 1
    )
    video_arrived = padded_2(video_edge.astype(jnp.bfloat16), (("tm", 1),), VBLK).astype(
        video_edge.dtype
    )
    video_kv_grad = settle(video_kv_ext, video_arrived, VBLK)
    audio_edge = jnp.concatenate(
        [audio_kv_ext[:, :edge_rows], audio_kv_ext[:, audio_kv_ext.shape[1] - edge_rows :]], 1
    )
    audio_arrived = padded_2(audio_edge.astype(jnp.bfloat16), (("tm", 1),), edge_rows).astype(
        audio_edge.dtype
    )
    audio_kv_grad = settle(audio_kv_ext, audio_arrived, edge_rows)
    returning = jnp.concatenate(
        [
            audio_q_grad[None].astype(jnp.bfloat16),
            audio_kv_grad.astype(jnp.bfloat16),
            audio_out[None],
        ],
        0,
    ).reshape(4, owners, audio_block, -1)
    returned = lax.all_to_all(returning, "tm", split_axis=1, concat_axis=1, tiled=True)
    audio_in = returned[:3]
    out_audio = returned[3]
    audio_in = lax.optimization_barrier(audio_in)
    video_raw = video_qkv[:2].astype(jnp.float32)
    audio_raw = audio_qkv[:2].astype(jnp.float32)
    video_in = jnp.stack([video_q_grad, video_kv_grad[0]])
    audio_wide = audio_in[:2].astype(jnp.float32)
    inner_sums = lax.psum(
        (
            jnp.sum(video_raw * video_gain[:, None, :] * video_in, -1),
            jnp.sum(audio_raw * audio_gain[:, None, None, :] * audio_wide, -1),
        ),
        "head",
    )
    video_back = (
        video_gain[:, None, :] * video_in * video_rate[..., None]
        - video_raw * (video_rate**3 * inner_sums[0] / feat_all)[..., None]
    )
    audio_back = (
        audio_gain[:, None, None, :] * audio_wide * audio_rate[..., None]
        - audio_raw * (audio_rate**3 * inner_sums[1] / feat_all)[..., None]
    )
    grad_video = jnp.concatenate([video_back, video_kv_grad[1:2]], 0).astype(jnp.bfloat16)
    grad_audio = jnp.concatenate([audio_back.astype(jnp.bfloat16), audio_in[2:3]], 0)
    return (out_video, out_audio, grad_video, grad_audio)


def solution(mesh):
    return jax.shard_map(
        local,
        mesh=mesh,
        in_specs=(
            P(None, "tm", "head"),
            P(None, None, "tm", "head"),
            P(None, "head"),
            P(None, "head"),
            P("tm", "head"),
            P(None, "tm", "head"),
            P(),
            P(),
        ),
        out_specs=(
            P("tm", "head"),
            P(None, "tm", "head"),
            P(None, "tm", "head"),
            P(None, None, "tm", "head"),
        ),
        check_vma=False,
    )
```

profile of v0, /device:TPU:34, one launch (start us, length us, event | category | flops | bytes accessed | tf_op | source)
XLA Modules:
  0.0 287.1 jit_solution(12065038965790831991)
XLA Ops:
  3.5 2.7 slice.146
  8.3 8.7 %all-reduce.6 = (f32[2,64,4]{1,2,0:T(4,128)S(1)}, f32[2,512]{1,0:T(2,128)S(1)}) all-reduce(f32[2,64,4]{1,2,0:T(4,128)S(1)} %copy.180, f32[2,512]{1,0:T(2,128)S(1)} %fusion.9), channel_id=1, replica_groups=mesh['tm'=64,'head'=4] {'head'}, use_global_device_ids=true, to_apply=%region_1.0 | all-reduce | flops 1536 | bytes 12288 | tf_op jit(solution)/shard_map/psum | solution.py:159
  18.3 3.3 %pad_maximum_fusion.5 = bf16[4,64,4,768]{3,2,0,1:T(4,128)(2,1)} fusion(bf16[1,64,4,768]{3,2,0,1:T(4,128)(2,1)} %bitcast.98, bf16[1,64,4,768]{3,2,0,1:T(4,128)(2,1)S(1)} %slice_bitcast_fusion.1, bf16[2,64,4,768]{3,2,0,1:T(4,128)(2,1)S(1)} %fusion.35), kind=kLoop, calls=%fused_computation.68 | loop fusion | flops 1572864 | bytes 3145728 | tf_op jit(solution)/shard_map/concatenate | solution.py:168
  21.6 12.1 %all-to-all-start = ((bf16[4,64,4,768]{3,2,0,1:T(4,128)(2,1)}), bf16[4,64,4,768]{3,2,0,1:T(4,128)(2,1)}, u32[]{:S(2)}, u32[]{:S(2)}) async-start(bf16[4,64,4,768]{3,2,0,1:T(4,128)(2,1)} %pad_maximum_fusion.5), calls=%async_computation | async-start | bytes 3145728 | tf_op jit(solution)/shard_map/all_to_all | solution.py:169
  39.3 5.6 %collective-permute-start.3 = (bf16[2,128,768]{1,2,0:T(8,128)(2,1)S(1)}, bf16[2,128,768]{1,2,0:T(8,128)(2,1)S(1)}, u32[]{:S(2)}, u32[]{:S(2)}) collective-permute-start(bf16[2,128,768]{1,2,0:T(8,128)(2,1)S(1)} %get-tuple-element.43), channel_id=1, source_target_pairs={{4,0},{8,4},{12,8},{16,12},{20,16},{24,20},{28,24},{32,28},{36,32}... | collective-permute-start | bytes 1179656 | tf_op jit(solution)/shard_map/ppermute | solution.py:24
  69.8 5.2 %collective-permute-done.2 = bf16[2,128,768]{1,2,0:T(8,128)(2,1)S(1)} collective-permute-done((bf16[2,128,768]{1,2,0:T(8,128)(2,1)}, bf16[2,128,768]{1,2,0:T(8,128)(2,1)S(1)}, u32[]{:S(2)}, u32[]{:S(2)}) %collective-permute-start.2) | collective-permute-done | bytes 393248 | tf_op jit(solution)/shard_map/ppermute | solution.py:23
  77.8 2.4 fusion.68
  89.4 6.0 %collective-permute-start.1 = (bf16[2,64,768]{2,0,1:T(2,128)(2,1)}, bf16[2,64,768]{2,0,1:T(2,128)(2,1)}, u32[]{:S(2)}, u32[]{:S(2)}) collective-permute-start(bf16[2,64,768]{2,0,1:T(2,128)(2,1)} %get-tuple-element.51), channel_id=1, source_target_pairs={{4,0},{8,4},{12,8},{16,12},{20,16},{24,20},{28,24},{32,28},{36,32}... | collective-permute-start | bytes 589832 | tf_op jit(solution)/shard_map/ppermute | solution.py:24
  95.9 5.7 %fusion.75 = (f32[6,256]{1,0:T(8,128)}, f32[6,256,768]{2,1,0:T(8,128)}) fusion(pred[256,768]{1,0:T(8,128)(4,1)} %compare_and_fusion, bf16[256,6,128]{0,2,1:T(8,128)(2,1)S(1)} %copy.208, bf16[768,6,128]{0,2,1:T(8,128)(2,1)S(1)} %bitcast.90), kind=kOutput, calls=%fused_computation.144 | convolution fusion | flops 306709248 | bytes 6494208 | tf_op jit(solution)/shard_map/sub | solution.py:37
  101.6 2.7 divide_convert_fusion
  108.0 3.5 %convert_element_type.129 = bf16[1,64,4,768]{3,0,2,1:T(2,128)(2,1)} reshape(bf16[256,6,128]{2,1,0:T(8,128)(2,1)} %copy.203) | data formatting | bytes 786432 | tf_op jit(solution)/shard_map/convert_element_type | solution.py:119
  117.6 3.5 %convert_element_type.128 = bf16[1,64,4,768]{3,0,2,1:T(2,128)(2,1)} reshape(bf16[256,6,128]{2,1,0:T(8,128)(2,1)} %copy.195) | data formatting | bytes 786432 | tf_op jit(solution)/shard_map/convert_element_type | solution.py:209
  121.1 2.6 pad_maximum_fusion.7
  123.8 2.6 fusion.71
  126.4 4.5 %copy.186 = bf16[1,384,768]{1,2,0:T(8,128)(2,1)} copy(bf16[1,384,768]{2,0,1:T(2,128)(2,1)} %get-tuple-element.48) | data formatting | bytes 1179648 | tf_op jit(solution)/shard_map/slice | solution.py:107
  130.9 3.0 %copy.184 = bf16[1,384,768]{1,2,0:T(8,128)(2,1)} copy(bf16[1,384,768]{2,0,1:T(2,128)(2,1)S(1)} %get-tuple-element.49) | data formatting | bytes 1179648 | tf_op jit(solution)/shard_map/slice | solution.py:108
  133.9 5.4 %fusion.74 = (f32[6,512]{1,0:T(8,128)S(1)}, f32[6,512,384]{1,2,0:T(8,128)}) fusion(pred[512,384]{0,1:T(8,128)(4,1)} %and_and_fusion, bf16[512,6,128]{0,2,1:T(8,128)(2,1)} %bitcast.94, bf16[384,6,128]{0,2,1:T(8,128)(2,1)} %bitcast.96), kind=kOutput, calls=%fused_computation.143 | convolution fusion | flops 306708864 | bytes 6303744 | tf_op jit(solution)/shard_map/sub | solution.py:37
  139.3 3.1 %divide_convert_fusion.1 = bf16[6,512,384]{1,2,0:T(8,128)(2,1)S(1)} fusion(f32[6,512,384]{1,2,0:T(8,128)} %get-tuple-element.55, f32[6,512]{1,0:T(8,128)S(1)} %get-tuple-element.54), kind=kLoop, calls=%fused_computation.22 | loop fusion | flops 2359296 | bytes 7090176 | tf_op jit(solution)/shard_map/convert_element_type | solution.py:38
  145.6 3.5 %copy.202 = f32[1,384,768]{2,0,1:T(1,128)S(1)} copy(f32[1,384,768]{1,2,0:T(8,128)} %bitcast.89) | data formatting | bytes 2359296 | tf_op jit(solution)/shard_map/stack;reshape | solution.py:127
  149.1 3.1 %fusion.5 = (f32[6,512]{1,0:T(8,128)S(1)}, f32[6,384,512]{2,1,0:T(8,128)S(1)}) fusion(bf16[6,512,384]{1,2,0:T(8,128)(2,1)} %copy-done, bf16[384,6,128]{0,2,1:T(8,128)(2,1)} %bitcast.84, bf16[512,6,128]{0,2,1:T(8,128)(2,1)} %bitcast.82), kind=kOutput, calls=%fused_computation.16 | convolution fusion | flops 305525760 | bytes 8466432 | tf_op jit(solution)/shard_map/qhe,khe->hqk/dot_general | solution.py:43
  156.4 12.9 %copy.201 = f32[1,384,768]{2,0,1:T(1,128)} copy(f32[1,384,768]{1,2,0:T(8,128)} %bitcast.88) | data formatting | bytes 2359296 | tf_op jit(solution)/shard_map/stack;reshape | solution.py:127
  169.3 3.5 %fusion.19 = bf16[2,384,768]{2,0,1:T(2,128)(2,1)S(1)} fusion(f32[1,384,768]{2,0,1:T(1,128)S(1)} %copy.202, f32[1,384,768]{2,0,1:T(1,128)} %copy.201), kind=kLoop, calls=%fused_computation.45 | loop fusion | flops 2359296 | bytes 3538944 | tf_op jit(solution)/shard_map/convert.9
  175.0 5.9 %collective-permute-start.5 = (bf16[2,64,768]{2,0,1:T(2,128)(2,1)S(1)}, bf16[2,64,768]{2,0,1:T(2,128)(2,1)S(1)}, u32[]{:S(2)}, u32[]{:S(2)}) collective-permute-start(bf16[2,64,768]{2,0,1:T(2,128)(2,1)S(1)} %get-tuple-element.47), channel_id=1, source_target_pairs={{4,0},{8,4},{12,8},{16,12},{20,16},{24,20},{28,24},{32,28},{36,32}... | collective-permute-start | bytes 589832 | tf_op jit(solution)/shard_map/ppermute | solution.py:24
  185.2 11.1 %fusion.36 = bf16[2,256,768]{2,0,1:T(2,128)(2,1)S(1)} fusion(f32[2,64,768]{2,0,1:T(2,128)S(1)} %slice.190, pred[256]{0:T(512)(128)(4,1)S(1)} %copy-done.46, f32[1,384,768]{2,0,1:T(1,128)S(1)} %copy.202, f32[1,384,768]{2,0,1:T(1,128)S(1)} %copy-done.13, bf16[2,64,768]{2,0,1:T(2,128)(2,1)S(1)} %collective-permute-done.5, ...), kind=kLoop, calls=%fused_computation.72 | loop fusion | flops 3538944 | bytes 4325632 | tf_op jit(solution)/shard_map/convert_element_type | solution.py:210
  196.3 2.7 pad_maximum_fusion.6
  200.8 13.1 %all-to-all-start.1 = ((bf16[4,64,4,768]{3,2,0,1:T(4,128)(2,1)}), bf16[4,64,4,768]{3,2,0,1:T(4,128)(2,1)}, u32[]{:S(2)}, u32[]{:S(2)}) async-start(bf16[4,64,4,768]{3,2,0,1:T(4,128)(2,1)} %copy.206), calls=%async_computation.1 | async-start | bytes 3145728 | tf_op jit(solution)/shard_map/all_to_all | solution.py:215
  219.8 5.8 %collective-permute-start.7 = (bf16[2,128,768]{1,2,0:T(8,128)(2,1)S(1)}, bf16[2,128,768]{1,2,0:T(8,128)(2,1)}, u32[]{:S(2)}, u32[]{:S(2)}) collective-permute-start(bf16[2,128,768]{1,2,0:T(8,128)(2,1)S(1)} %get-tuple-element.37), channel_id=1, source_target_pairs={{4,0},{8,4},{12,8},{16,12},{20,16},{24,20},{28,24},{32,28},{36,32}... | collective-permute-start | bytes 1179656 | tf_op jit(solution)/shard_map/ppermute | solution.py:24
  229.4 2.4 convolution_multiply_fusion.1
  231.9 23.3 %collective-permute-done.6 = bf16[2,128,768]{1,2,0:T(8,128)(2,1)S(1)} collective-permute-done((bf16[2,128,768]{1,2,0:T(8,128)(2,1)S(1)}, bf16[2,128,768]{1,2,0:T(8,128)(2,1)S(1)}, u32[]{:S(2)}, u32[]{:S(2)}) %collective-permute-start.6) | collective-permute-done | bytes 393248 | tf_op jit(solution)/shard_map/ppermute | solution.py:23
  262.7 2.3 fusion.29
  265.1 10.8 %all-reduce.5 = (f32[2,512]{1,0:T(2,128)S(1)}, f32[2,64,4]{1,2,0:T(4,128)}) all-reduce(f32[2,512]{1,0:T(2,128)S(1)} %fusion.13, f32[2,64,4]{1,2,0:T(4,128)S(1)} %copy.210), channel_id=1, replica_groups=mesh['tm'=64,'head'=4] {'head'}, use_global_device_ids=true, to_apply=%region_11.12 | all-reduce | flops 1536 | bytes 12288 | tf_op jit(solution)/shard_map/psum | solution.py:223
  278.3 2.4 copy.213
  (195 shorter events, 99.9 us)
Async XLA Ops:
  6.2 11.6 %copy-start.14 = (bf16[3,64,4,768]{3,2,1,0:T(4,128)(2,1)S(1)}, bf16[3,64,4,768]{3,2,1,0:T(4,128)(2,1)}, u32[]{:S(2)}) copy-start(bf16[3,64,4,768]{3,2,1,0:T(4,128)(2,1)} %param.9) | copy-start | bytes 3538948
  6.2 11.6 %copy-start.33 = (f32[2,768]{1,0:T(2,128)S(1)}, f32[2,768]{1,0:T(2,128)}, u32[]{:S(2)}) copy-start(f32[2,768]{1,0:T(2,128)} %param.11) | copy-start | bytes 18436
  8.0 25.7 %copy-start.3 = (bf16[2,512,768]{1,2,0:T(8,128)(2,1)}, bf16[2,512,768]{1,2,0:T(8,128)(2,1)S(1)}, u32[]{:S(2)}) copy-start(bf16[2,512,768]{1,2,0:T(8,128)(2,1)S(1)} %copy.227) | copy-start | bytes 4718596
  17.1 16.6 %copy-start.39 = (f32[2,512]{1,0:T(2,128)}, f32[2,512]{1,0:T(2,128)S(1)}, u32[]{:S(2)}) copy-start(f32[2,512]{1,0:T(2,128)S(1)} %get-tuple-element.35) | copy-start | bytes 12292
  21.6 12.7 %copy-start.32 = (f32[2,768]{1,0:T(2,128)S(1)}, f32[2,768]{1,0:T(2,128)}, u32[]{:S(2)}) copy-start(f32[2,768]{1,0:T(2,128)} %param.10) | copy-start | bytes 18436
  21.6 53.7 %all-to-all-start = ((bf16[4,64,4,768]{3,2,0,1:T(4,128)(2,1)}), bf16[4,64,4,768]{3,2,0,1:T(4,128)(2,1)}, u32[]{:S(2)}, u32[]{:S(2)}) async-start(bf16[4,64,4,768]{3,2,0,1:T(4,128)(2,1)} %pad_maximum_fusion.5), calls=%async_computation | async-start | bytes 3145728 | tf_op jit(solution)/shard_map/all_to_all | solution.py:169
  36.1 30.9 %copy-start.30 = (bf16[512,768]{1,0:T(8,128)(2,1)S(1)}, bf16[512,768]{1,0:T(8,128)(2,1)}, u32[]{:S(2)}) copy-start(bf16[512,768]{1,0:T(8,128)(2,1)} %param.12) | copy-start | bytes 2359300
  37.3 37.6 %collective-permute-start.2 = (bf16[2,128,768]{1,2,0:T(8,128)(2,1)}, bf16[2,128,768]{1,2,0:T(8,128)(2,1)S(1)}, u32[]{:S(2)}, u32[]{:S(2)}) collective-permute-start(bf16[2,128,768]{1,2,0:T(8,128)(2,1)} %get-tuple-element.42), channel_id=1, source_target_pairs={{0,4},{4,8},{8,12},{12,16},{16,20},{20,24},{24,28},{28,32},{32,36}... | collective-permute-start | bytes 1179656 | tf_op jit(solution)/shard_map/ppermute | solution.py:23
  39.3 35.6 %collective-permute-start.3 = (bf16[2,128,768]{1,2,0:T(8,128)(2,1)S(1)}, bf16[2,128,768]{1,2,0:T(8,128)(2,1)S(1)}, u32[]{:S(2)}, u32[]{:S(2)}) collective-permute-start(bf16[2,128,768]{1,2,0:T(8,128)(2,1)S(1)} %get-tuple-element.43), channel_id=1, source_target_pairs={{4,0},{8,4},{12,8},{16,12},{20,16},{24,20},{28,24},{32,28},{36,32}... | collective-permute-start | bytes 1179656 | tf_op jit(solution)/shard_map/ppermute | solution.py:24
  75.3 20.6 %copy-start.21 = (bf16[1,768,768]{1,2,0:T(8,128)(2,1)}, bf16[1,768,768]{1,2,0:T(8,128)(2,1)S(1)}, u32[]{:S(2)}) copy-start(bf16[1,768,768]{1,2,0:T(8,128)(2,1)S(1)} %get-tuple-element.38) | copy-start | bytes 3538948
  77.8 9.7 %copy-start.19 = (bf16[2,64,4,768]{3,0,2,1:T(2,128)(2,1)}, bf16[2,64,4,768]{3,0,2,1:T(2,128)(2,1)S(1)}, u32[]{:S(2)}) copy-start(bf16[2,64,4,768]{3,0,2,1:T(2,128)(2,1)S(1)} %copy.183) | copy-start | bytes 2359300
  87.5 33.6 %collective-permute-start = (bf16[2,64,768]{2,0,1:T(2,128)(2,1)}, bf16[2,64,768]{2,0,1:T(2,128)(2,1)}, u32[]{:S(2)}, u32[]{:S(2)}) collective-permute-start(bf16[2,64,768]{2,0,1:T(2,128)(2,1)} %get-tuple-element.50), channel_id=1, source_target_pairs={{0,4},{4,8},{8,12},{12,16},{16,20},{20,24},{24,28},{28,32},{32,36}... | collective-permute-start | bytes 589832 | tf_op jit(solution)/shard_map/ppermute | solution.py:23
  89.4 31.7 %collective-permute-start.1 = (bf16[2,64,768]{2,0,1:T(2,128)(2,1)}, bf16[2,64,768]{2,0,1:T(2,128)(2,1)}, u32[]{:S(2)}, u32[]{:S(2)}) collective-permute-start(bf16[2,64,768]{2,0,1:T(2,128)(2,1)} %get-tuple-element.51), channel_id=1, source_target_pairs={{4,0},{8,4},{12,8},{16,12},{20,16},{24,20},{28,24},{32,28},{36,32}... | collective-permute-start | bytes 589832 | tf_op jit(solution)/shard_map/ppermute | solution.py:24
  169.3 11.6 %copy-start.25 = (bf16[1,64,4,768]{3,0,2,1:T(2,128)(2,1)S(1)}, bf16[1,64,4,768]{3,0,2,1:T(2,128)(2,1)}, u32[]{:S(2)}) copy-start(bf16[1,64,4,768]{3,0,2,1:T(2,128)(2,1)} %convert_element_type.129) | copy-start | bytes 1179652
  169.3 11.6 %copy-start.36 = (pred[64,4]{1,0:T(8,128)(4,1)S(1)}, pred[64,4]{1,0:T(8,128)(4,1)}, u32[]{:S(2)}) copy-start(pred[64,4]{1,0:T(8,128)(4,1)} %fusion.44) | copy-start | bytes 772
  173.1 9.1 %collective-permute-start.4 = (bf16[2,64,768]{2,0,1:T(2,128)(2,1)S(1)}, bf16[2,64,768]{2,0,1:T(2,128)(2,1)S(1)}, u32[]{:S(2)}, u32[]{:S(2)}) collective-permute-start(bf16[2,64,768]{2,0,1:T(2,128)(2,1)S(1)} %get-tuple-element.46), channel_id=1, source_target_pairs={{0,4},{4,8},{8,12},{12,16},{16,20},{20,24},{24,28},{28,32},{32,36}... | collective-permute-start | bytes 589832 | tf_op jit(solution)/shard_map/ppermute | solution.py:23
  175.0 10.2 %copy-start.13 = (f32[1,384,768]{2,0,1:T(1,128)S(1)}, f32[1,384,768]{2,0,1:T(1,128)}, u32[]{:S(2)}) copy-start(f32[1,384,768]{2,0,1:T(1,128)} %copy.201) | copy-start | bytes 3538948
  175.0 10.2 %copy-start.46 = (pred[256]{0:T(512)(128)(4,1)S(1)}, pred[256]{0:T(512)(128)(4,1)}, u32[]{:S(2)}) copy-start(pred[256]{0:T(512)(128)(4,1)} %constant.92.clone.1) | copy-start | bytes 772
  175.0 9.1 %collective-permute-start.5 = (bf16[2,64,768]{2,0,1:T(2,128)(2,1)S(1)}, bf16[2,64,768]{2,0,1:T(2,128)(2,1)S(1)}, u32[]{:S(2)}, u32[]{:S(2)}) collective-permute-start(bf16[2,64,768]{2,0,1:T(2,128)(2,1)S(1)} %get-tuple-element.47), channel_id=1, source_target_pairs={{4,0},{8,4},{12,8},{16,12},{20,16},{24,20},{28,24},{32,28},{36,32}... | collective-permute-start | bytes 589832 | tf_op jit(solution)/shard_map/ppermute | solution.py:24
  185.2 11.1 %copy-start.26 = (bf16[1,64,4,768]{3,0,2,1:T(2,128)(2,1)S(1)}, bf16[1,64,4,768]{3,0,2,1:T(2,128)(2,1)}, u32[]{:S(2)}) copy-start(bf16[1,64,4,768]{3,0,2,1:T(2,128)(2,1)} %convert_element_type.128) | copy-start | bytes 1179652
  200.8 13.1 %copy-start.23 = (bf16[256,6,128]{0,2,1:T(8,128)(2,1)S(1)}, bf16[256,6,128]{0,2,1:T(8,128)(2,1)}, u32[]{:S(2)}) copy-start(bf16[256,6,128]{0,2,1:T(8,128)(2,1)} %copy.209) | copy-start | bytes 1179652
  200.8 60.1 %all-to-all-start.1 = ((bf16[4,64,4,768]{3,2,0,1:T(4,128)(2,1)}), bf16[4,64,4,768]{3,2,0,1:T(4,128)(2,1)}, u32[]{:S(2)}, u32[]{:S(2)}) async-start(bf16[4,64,4,768]{3,2,0,1:T(4,128)(2,1)} %copy.206), calls=%async_computation.1 | async-start | bytes 3145728 | tf_op jit(solution)/shard_map/all_to_all | solution.py:215
  217.0 8.6 %copy-start.2 = (bf16[6,512,384]{1,2,0:T(8,128)(2,1)S(1)}, bf16[6,512,384]{1,2,0:T(8,128)(2,1)}, u32[]{:S(2)}) copy-start(bf16[6,512,384]{1,2,0:T(8,128)(2,1)} %copy-done) | copy-start | bytes 7077892
  217.0 8.6 %copy-start.18 = (bf16[1,384,768]{1,2,0:T(8,128)(2,1)S(1)}, bf16[1,384,768]{1,2,0:T(8,128)(2,1)}, u32[]{:S(2)}) copy-start(bf16[1,384,768]{1,2,0:T(8,128)(2,1)} %copy.184) | copy-start | bytes 1769476
  217.6 37.6 %collective-permute-start.6 = (bf16[2,128,768]{1,2,0:T(8,128)(2,1)S(1)}, bf16[2,128,768]{1,2,0:T(8,128)(2,1)S(1)}, u32[]{:S(2)}, u32[]{:S(2)}) collective-permute-start(bf16[2,128,768]{1,2,0:T(8,128)(2,1)S(1)} %get-tuple-element.36), channel_id=1, source_target_pairs={{0,4},{4,8},{8,12},{12,16},{16,20},{20,24},{24,28},{28,32},{32,36}... | collective-permute-start | bytes 1179656 | tf_op jit(solution)/shard_map/ppermute | solution.py:23
  219.8 35.4 %collective-permute-start.7 = (bf16[2,128,768]{1,2,0:T(8,128)(2,1)S(1)}, bf16[2,128,768]{1,2,0:T(8,128)(2,1)}, u32[]{:S(2)}, u32[]{:S(2)}) collective-permute-start(bf16[2,128,768]{1,2,0:T(8,128)(2,1)S(1)} %get-tuple-element.37), channel_id=1, source_target_pairs={{4,0},{8,4},{12,8},{16,12},{20,16},{24,20},{28,24},{32,28},{36,32}... | collective-permute-start | bytes 1179656 | tf_op jit(solution)/shard_map/ppermute | solution.py:24
  231.8 27.3 %copy-start.10 = (f32[6,128,512]{2,1,0:T(8,128)}, f32[6,128,512]{2,1,0:T(8,128)S(1)}, u32[]{:S(2)}) copy-start(f32[6,128,512]{2,1,0:T(8,128)S(1)} %convolution_multiply_fusion.1) | copy-start | bytes 4718596
  231.9 24.6 %copy-start.6 = (f32[6,128,768]{2,1,0:T(8,128)S(1)}, f32[6,128,768]{2,1,0:T(8,128)}, u32[]{:S(2)}) copy-start(f32[6,128,768]{2,1,0:T(8,128)} %copy-done.5) | copy-start | bytes 7077892
  231.9 24.6 %copy-start.45 = (pred[512]{0:T(512)(128)(4,1)S(1)}, pred[512]{0:T(512)(128)(4,1)}, u32[]{:S(2)}) copy-start(pred[512]{0:T(512)(128)(4,1)} %constant.93.clone.1) | copy-start | bytes 1540
  260.8 15.1 %copy-start.40 = (f32[2,512]{1,0:T(2,128)S(1)}, f32[2,512]{1,0:T(2,128)}, u32[]{:S(2)}) copy-start(f32[2,512]{1,0:T(2,128)} %copy-done.39) | copy-start | bytes 12292
  260.9 15.1 %copy-start.11 = (f32[6,128,512]{2,1,0:T(8,128)S(1)}, f32[6,128,512]{2,1,0:T(8,128)}, u32[]{:S(2)}) copy-start(f32[6,128,512]{2,1,0:T(8,128)} %copy-done.10) | copy-start | bytes 4718596
  260.9 15.1 %copy-start.35 = (f32[2,512]{1,0:T(2,128)S(1)}, f32[2,512]{1,0:T(2,128)}, u32[]{:S(2)}) copy-start(f32[2,512]{1,0:T(2,128)} %copy-done.34) | copy-start | bytes 12292
  (27 other events, 59.3 us)
where the time goes:
time: 293 us; the launch traced here: 287 us
  local copies, waits for them, and re-layouts  96.1 us (33%)
  starting transfers between devices  56.6 us (19%)
  other arithmetic  55.4 us (19%)
  waiting for transfers between devices  30.5 us (10%)
  matrix products  27.2 us (9%)
  blocking collectives  19.5 us (7%)
    ppermute x4, waiting for transfers between devices, padded_2(): before = lax.ppermute(last, axis, up)  28.6 us
    ppermute x4, starting transfers between devices, padded_2(): after = lax.ppermute(first, axis, down)  23.3 us
    unnamed x101, local copies, waits for them, and re-layouts  19.8 us
    another operation x2, local copies, waits for them, and re-layouts, cross_window(): jnp.stack([to_rows(dk_audio), to_rows(dv_audio)])  16.4 us
    all_to_all x1, starting transfers between devices, local(): lax.all_to_all(returning, 'tm', split_axis=1, concat_axis=1, tiled=True)  13.1 us
    all_to_all x1, starting transfers between devices, local(): lax.all_to_all(outgoing, 'tm', split_axis=1, concat_axis=1, tiled=True)  12.1 us
    convert_element_type x1, other arithmetic, local(): audio_kv_grad.astype(jnp.bfloat16)  11.1 us
    sub x2, matrix products, attend(): exponent = jnp.exp(scores - row_max)  11.1 us
  transfers between devices with their start and end apart: 10, of which 4 were waited for; matrix products, arithmetic and copies ran while one was open for 23% of the time, Pallas kernels for 0%

commit v1 on v0

v1 whole, which is shorter than its diff:
```python
import functools

import jax
import jax.numpy as jnp
from jax import lax
from jax.experimental import pallas as pl
from jax.experimental.pallas import tpu as pltpu
from jax.sharding import PartitionSpec as P

HEADS = 24
HD = 128
VB = 4
VBLK = 128
CHUNKS = 3

EPSILON = 1e-06
NEGATIVE = -1e30
MESH = pl.DeviceIdType.MESH
F32 = jnp.float32
BF16 = jnp.bfloat16


def mm(a, b, ca, cb):
    return lax.dot_general(a, b, (((ca,), (cb,)), ((), ())), preferred_element_type=F32)


def attend(query, key, value, cot, bias):
    scale = HD ** (-0.5)
    scores = mm(key, query, 1, 1) * scale + bias
    exponent = jnp.exp(scores - jnp.max(scores, 0, keepdims=True))
    inverse = 1.0 / jnp.sum(exponent, 0, keepdims=True)
    probs = (exponent * inverse).astype(BF16)
    wide = probs.astype(F32)
    prob_grad = mm(value, cot, 1, 1)
    inner = jnp.sum(prob_grad * wide, 0, keepdims=True)
    score_grad = (wide * (prob_grad - inner)).astype(BF16)
    out = mm(probs, value, 0, 0)
    query_grad = mm(score_grad, key, 0, 0) * scale
    key_grad = mm(score_grad, query, 1, 0) * scale
    value_grad = mm(probs, cot, 1, 0)
    return out, query_grad, key_grad, value_grad


def iota(shape, dim):
    return lax.broadcasted_iota(jnp.int32, shape, dim)


def to_row(column):
    n = column.shape[0]
    return jnp.sum(jnp.where(iota((n, 128), 0) == iota((n, 128), 1), column, 0.0), 0, keepdims=True)


def to_column(row, n):
    return jnp.sum(jnp.where(iota((n, 128), 0) == iota((n, 128), 1), row, 0.0), 1, keepdims=True)


def kernel(
    dims,
    vq_hbm, aq_hbm, vg, ag, vc_hbm, ac_hbm, inter, lens,
    ov_hbm, oa, gv_hbm, ga,
    vraw, vcot, araw, acot, vqn, vkv, msg, win, aqn, akv, acw,
    ov, dqv, dvkv, dqa, dakv, oaw, evs, evr, eas, ear, ret, retr, aun, gv,
    vab, avb, live, stats, rates, inner,
    in_sem, out_sem, st_send, st_recv, vh_send, vh_recv, ah_send, ah_recv,
    a2a_send, a2a_recv, ev_send, ev_recv, ea_send, ea_recv, ret_send, ret_recv,
):
    n, x, f = dims
    c_all, w = CHUNKS, f // CHUNKS
    heads = w // HD
    tok = 4
    nb = n // VB
    ga_rows = nb * tok
    a_rows = n * tok
    ae_rows = a_rows + 2 * ga_rows
    v_rows = VB * VBLK
    lv, la = min(128, v_rows), min(128, a_rows)
    nv, na = v_rows // lv, a_rows // la
    blocks = n * n
    feat_all = HEADS * HD
    me = lax.axis_index("tm")
    hd = lax.axis_index("head")
    left, right = lax.rem(me + n - 1, n), lax.rem(me + 1, n)

    barrier = pltpu.get_barrier_semaphore()
    for k in range(1, x):
        pl.semaphore_signal(barrier, inc=1, device_id={"head": lax.rem(hd + k, x)}, device_id_type=MESH)

    def greet(k, carry):
        pl.semaphore_signal(barrier, inc=1, device_id={"tm": lax.rem(me + k, n)}, device_id_type=MESH)
        return carry

    loads = [
        pltpu.make_async_copy(vq_hbm.at[pl.ds(0, 2)], vraw, in_sem.at[0]),
        pltpu.make_async_copy(aq_hbm, araw, in_sem.at[1]),
        pltpu.make_async_copy(ac_hbm, acot, in_sem.at[2]),
        pltpu.make_async_copy(vq_hbm.at[2], vkv.at[1, pl.ds(VBLK, v_rows)], in_sem.at[3]),
        pltpu.make_async_copy(vc_hbm, vcot, in_sem.at[4]),
    ]
    for load in loads:
        load.start()
    lax.fori_loop(1, n, greet, 0)

    start = me * n - nb
    count = blocks // 128
    chunk_0 = lax.rem((start + blocks) // 128, count)
    chunk_1 = lax.rem(chunk_0 + 1, count)
    rows = iota((ae_rows, 1), 0)
    block = start + lax.shift_right_logical(rows, 2)
    block = jnp.where(block < 0, block + blocks, block)
    block = jnp.where(block >= blocks, block - blocks, block)
    tables = []
    for ref, at in ((inter, 0), (inter, 1), (lens, 0)):
        column = jnp.zeros((ae_rows, 1), F32)
        for chunk in (chunk_0, chunk_1):
            lanes = pl.ds(pl.multiple_of(chunk * 128, 128), 128)
            values = ref[at : at + 1, lanes].astype(F32)
            hit = (chunk * 128 + iota((ae_rows, 128), 1)) == block
            column = column + jnp.sum(jnp.where(hit, values, 0.0), 1, keepdims=True)
        tables.append(column)
    low, high, length = tables
    is_live = jnp.bitwise_and(rows, 3).astype(F32) < length
    first = (me * VB).astype(F32)
    for b in range(VB):
        span = slice(b * ga_rows, (b + 3) * ga_rows)
        ok = (low[span] <= first + b) & (first + b <= high[span]) & is_live[span]
        vab[b] = jnp.broadcast_to(jnp.where(ok, 0.0, NEGATIVE), (3 * ga_rows, VBLK))
    pair = 2 * ga_rows
    for p in range(2):
        span = slice(ga_rows + p * pair, ga_rows + (p + 1) * pair)
        low_row = to_row(low[span])[:, :pair]
        high_row = to_row(high[span])[:, :pair]
        for e in range(4):
            at = first + (2 * p + e - 1)
            ok = (low_row <= at) & (at <= high_row)
            avb[p, e * VBLK : (e + 1) * VBLK] = jnp.broadcast_to(
                jnp.where(ok, 0.0, NEGATIVE), (VBLK, pair)
            )
    live[...] = jnp.broadcast_to(
        jnp.where(is_live[ga_rows : ga_rows + a_rows], 1.0, 0.0), (a_rows, 128)
    )

    stats[0, hd] = jnp.zeros((16, 128), F32)
    loads[1].wait()
    for p in range(2):
        for i in range(na):
            cut = slice(i * la // tok, (i + 1) * la // tok)
            raw = araw[p, cut].reshape(la, f).astype(F32)
            at = 2 * nv + p * na + i
            stats[0, hd, at : at + 1] = to_row(jnp.sum(raw * raw, 1, keepdims=True))
    loads[0].wait()
    for p in range(2):
        for i in range(nv):
            raw = vraw[p, i * lv : (i + 1) * lv].astype(F32)
            at = p * nv + i
            stats[0, hd, at : at + 1] = to_row(jnp.sum(raw * raw, 1, keepdims=True))
    loads[2].wait()
    loads[3].wait()
    loads[4].wait()

    def share(turn):
        copies = []
        for k in range(1, x):
            copies.append(
                pltpu.make_async_remote_copy(
                    stats.at[turn, hd], stats.at[turn, hd],
                    st_send.at[turn], st_recv.at[turn],
                    device_id={"head": lax.rem(hd + k, x)}, device_id_type=MESH,
                )
            )
        for copy in copies:
            copy.start()

    def shared(turn):
        some = stats.at[turn, pl.ds(0, x - 1)]
        pltpu.make_async_copy(some, some, st_recv.at[turn]).wait()
        pltpu.make_async_copy(some, some, st_send.at[turn]).wait()
        total = stats[turn, 0]
        for k in range(1, x):
            total = total + stats[turn, k]
        return total

    def edge_copy(src, dst, send, recv, to):
        return pltpu.make_async_remote_copy(
            src, dst, send, recv, device_id={"tm": to}, device_id_type=MESH
        )

    pl.semaphore_wait(barrier, n - 1 + x - 1)
    share(0)

    def video_halo(kind):
        return (
            edge_copy(vkv.at[kind, pl.ds(VBLK, VBLK)], vkv.at[kind, pl.ds(VBLK + v_rows, VBLK)],
                      vh_send.at[kind, 0], vh_recv.at[kind, 0], left),
            edge_copy(vkv.at[kind, pl.ds(v_rows, VBLK)], vkv.at[kind, pl.ds(0, VBLK)],
                      vh_send.at[kind, 1], vh_recv.at[kind, 1], right),
        )

    for copy in video_halo(1):
        copy.start()
    rates[...] = lax.rsqrt(shared(0) / feat_all + EPSILON)

    size = 4 * ga_rows
    one, two = iota((size, size), 0), iota((size, size), 1)

    def moved(row):
        arr = lax.rem(lax.div(row, tok), 4)
        return arr * ga_rows + lax.div(row, 4 * tok) * tok + lax.rem(row, tok)

    pack = jnp.where(two == moved(one), 1.0, 0.0).astype(BF16)
    unpack = jnp.where(one == moved(two), 1.0, 0.0).astype(BF16)

    def audio_rate(p, row_at, row_count):
        i, off = divmod(row_at, la)
        at = 2 * nv + p * na + i
        return to_column(rates[at : at + 1], la)[off : off + row_count]

    for j in range(VB):
        cut = slice(j * nb, (j + 1) * nb)
        parts = []
        for p in range(2):
            raw = araw[p, cut].reshape(ga_rows, f).astype(F32)
            normed = raw * audio_rate(p, j * ga_rows, ga_rows) * ag[p : p + 1]
            parts.append(normed.astype(BF16))
        parts.append(araw[2, cut].reshape(ga_rows, f))
        parts.append(acot[cut].reshape(ga_rows, f))
        packed = mm(pack, jnp.concatenate(parts, 0), 1, 0).astype(BF16)
        msg[cut] = packed.reshape(nb, 16, f)

    def lanes_of(c):
        return pl.ds(pl.multiple_of(c * w, w), w)

    def spread(src, dst, send, recv):
        def chunk(c, carry):
            lanes = lanes_of(c)

            def one_device(k, inner_carry):
                d = lax.rem(me + k, n)
                edge_copy(src.at[d, :, lanes], dst.at[me, :, lanes], send.at[c], recv.at[c], d).start()
                return inner_carry

            lax.fori_loop(1, n, one_device, 0)
            pltpu.make_async_copy(src.at[me, :, lanes], dst.at[me, :, lanes], recv.at[c]).start()
            return carry

        return chunk

    def landed(dst, recv, c):
        some = dst.at[:, :, lanes_of(c)]
        pltpu.make_async_copy(some, some, recv.at[c]).wait()

    def sent(src, send, c):
        some = src.at[pl.ds(0, n - 1), :, lanes_of(c)]
        pltpu.make_async_copy(some, some, send.at[c]).wait()

    lax.fori_loop(0, c_all, spread(msg, win, a2a_send, a2a_recv), 0)

    for p in (1, 0):
        for i in range(nv):
            cut = slice(i * lv, (i + 1) * lv)
            at = p * nv + i
            raw = vraw[p, cut].astype(F32)
            normed = (raw * to_column(rates[at : at + 1], lv) * vg[p : p + 1]).astype(BF16)
            if p == 1:
                vkv[0, VBLK + i * lv : VBLK + (i + 1) * lv] = normed
            else:
                vqn[cut] = normed
        if p == 1:
            for copy in video_halo(0):
                copy.start()

    def audio_halo(c):
        lanes = lanes_of(c)
        return (
            edge_copy(akv.at[:, pl.ds(ga_rows, ga_rows), lanes],
                      akv.at[:, pl.ds(ga_rows + a_rows, ga_rows), lanes],
                      ah_send.at[c, 0], ah_recv.at[c, 0], left),
            edge_copy(akv.at[:, pl.ds(a_rows, ga_rows), lanes],
                      akv.at[:, pl.ds(0, ga_rows), lanes],
                      ah_send.at[c, 1], ah_recv.at[c, 1], right),
        )

    def grad_halo(src, dst, send, recv, c):
        lanes = lanes_of(c)
        return (
            edge_copy(src.at[0, :, :, lanes], dst.at[1, :, :, lanes], send.at[c, 0], recv.at[c, 0], left),
            edge_copy(src.at[1, :, :, lanes], dst.at[0, :, :, lanes], send.at[c, 1], recv.at[c, 1], right),
        )

    spread_back = spread(ret, retr, ret_send, ret_recv)

    def finish(c):
        lanes = lanes_of(c)
        for copy in grad_halo(eas, ear, ea_send, ea_recv, c):
            copy.wait_recv()
        for j in range(VB):
            cut = slice(j * ga_rows, (j + 1) * ga_rows)
            parts = [dqa[cut, lanes]]
            for kind in range(2):
                total = dakv[kind, (j + 1) * ga_rows : (j + 2) * ga_rows, lanes]
                if j == 0:
                    total = total + ear[0, kind, :, lanes].astype(F32)
                if j == VB - 1:
                    total = total + ear[1, kind, :, lanes].astype(F32)
                parts.append(total.astype(BF16))
            parts.append(oaw[cut, lanes])
            packed = mm(pack, jnp.concatenate(parts, 0), 1, 0).astype(BF16)
            ret[j * nb : (j + 1) * nb, :, lanes] = packed.reshape(nb, 16, w)
        spread_back(c, 0)

    def chunk_work(c, carry):
        lanes = lanes_of(c)
        landed(win, a2a_recv, c)
        for j in range(VB):
            some = win[j * nb : (j + 1) * nb, :, lanes].reshape(size, w)
            some = mm(unpack, some, 1, 0)
            cut = slice(j * ga_rows, (j + 1) * ga_rows)
            ext = slice((j + 1) * ga_rows, (j + 2) * ga_rows)
            aqn[cut, lanes] = some[:ga_rows].astype(BF16)
            akv[0, ext, lanes] = some[ga_rows : 2 * ga_rows].astype(BF16)
            akv[1, ext, lanes] = some[2 * ga_rows : 3 * ga_rows].astype(BF16)
            acw[cut, lanes] = jnp.where(live[cut, :1] > 0.0, some[3 * ga_rows :], 0.0).astype(BF16)
        for copy in audio_halo(c):
            copy.start()

        @pl.when(c == 0)
        def _():
            for kind in range(2):
                for copy in video_halo(kind):
                    copy.wait_recv()

        for h in range(heads):
            at = pl.ds(pl.multiple_of(c * w + h * HD, HD), HD)
            sums = [[None] * 6, [None] * 6]
            for p in range(2):
                cut = slice(p * pair, (p + 1) * pair)
                ext = slice(2 * p * VBLK, (2 * p + 4) * VBLK)
                out, dq, dk, dv = attend(
                    aqn[cut, at], vkv[0, ext, at], vkv[1, ext, at], acw[cut, at], avb[p]
                )
                oaw[cut, at] = jnp.where(live[cut, :1] > 0.0, out, 0.0).astype(BF16)
                dqa[cut, at] = dq.astype(BF16)
                for kind, grad in enumerate((dk, dv)):
                    for e in range(4):
                        term = grad[e * VBLK : (e + 1) * VBLK]
                        old = sums[kind][2 * p + e]
                        sums[kind][2 * p + e] = term if old is None else old + term
            for kind in range(2):
                evs[0, kind, :, at] = sums[kind][0].astype(BF16)
                evs[1, kind, :, at] = sums[kind][5].astype(BF16)
                for e in range(4):
                    dvkv[kind, e * VBLK : (e + 1) * VBLK, at] = sums[kind][e + 1]
        for copy in grad_halo(evs, evr, ev_send, ev_recv, c):
            copy.start()
        for copy in audio_halo(c):
            copy.wait_recv()
        for h in range(heads):
            at = pl.ds(pl.multiple_of(c * w + h * HD, HD), HD)
            sums = [[None] * 6, [None] * 6]
            for b in range(VB):
                cut = slice(b * VBLK, (b + 1) * VBLK)
                ext = slice(b * ga_rows, (b + 3) * ga_rows)
                out, dq, dk, dv = attend(
                    vqn[cut, at], akv[0, ext, at], akv[1, ext, at], vcot[cut, at], vab[b]
                )
                ov[cut, at] = out.astype(BF16)
                dqv[cut, at] = dq
                for kind, grad in enumerate((dk, dv)):
                    for e in range(3):
                        term = grad[e * ga_rows : (e + 1) * ga_rows]
                        old = sums[kind][b + e]
                        sums[kind][b + e] = term if old is None else old + term
            for kind in range(2):
                eas[0, kind, :, at] = sums[kind][0].astype(BF16)
                eas[1, kind, :, at] = sums[kind][5].astype(BF16)
                for e in range(4):
                    dakv[kind, (e + 1) * ga_rows : (e + 2) * ga_rows, at] = sums[kind][e + 1]
        for copy in grad_halo(eas, ear, ea_send, ea_recv, c):
            copy.start()

        @pl.when(c > 0)
        def _():
            finish(c - 1)

        return carry

    lax.fori_loop(0, c_all, chunk_work, 0)
    put_ov = pltpu.make_async_copy(ov, ov_hbm, out_sem.at[0])
    put_ov.start()
    finish(c_all - 1)

    def wait_edges(c, carry):
        for copy in grad_halo(evs, evr, ev_send, ev_recv, c):
            copy.wait_recv()
        return carry

    lax.fori_loop(0, c_all, wait_edges, 0)
    for kind in range(2):
        head_rows, tail_rows = slice(0, VBLK), slice(v_rows - VBLK, v_rows)
        dvkv[kind, head_rows] = dvkv[kind, head_rows] + evr[0, kind].astype(F32)
        dvkv[kind, tail_rows] = dvkv[kind, tail_rows] + evr[1, kind].astype(F32)
    stats[1, hd] = jnp.zeros((16, 128), F32)
    for p in range(2):
        for i in range(nv):
            cut = slice(i * lv, (i + 1) * lv)
            grad = dqv[cut] if p == 0 else dvkv[0, cut]
            term = vraw[p, cut].astype(F32) * vg[p : p + 1] * grad
            at = p * nv + i
            stats[1, hd, at : at + 1] = to_row(jnp.sum(term, 1, keepdims=True))
    share(1)
    for i in range(nv):
        cut = slice(i * lv, (i + 1) * lv)
        gv[2, cut] = dvkv[1, cut].astype(BF16)
    inner[...] = rates[...] * rates[...] * rates[...] * shared(1) / feat_all
    for p in range(2):
        for i in range(nv):
            cut = slice(i * lv, (i + 1) * lv)
            at = p * nv + i
            grad = dqv[cut] if p == 0 else dvkv[0, cut]
            rate = to_column(rates[at : at + 1], lv)
            back = vg[p : p + 1] * grad * rate - vraw[p, cut].astype(F32) * to_column(inner[at : at + 1], lv)
            gv[p, cut] = back.astype(BF16)
    put_gv = pltpu.make_async_copy(gv, gv_hbm, out_sem.at[1])
    put_gv.start()

    def take(c, carry):
        lanes = lanes_of(c)
        landed(retr, ret_recv, c)
        for j in range(VB):
            some = retr[j * nb : (j + 1) * nb, :, lanes].reshape(size, w)
            some = mm(unpack, some, 1, 0).astype(BF16)
            for arr in range(4):
                aun[arr, j * ga_rows : (j + 1) * ga_rows, lanes] = some[arr * ga_rows : (arr + 1) * ga_rows]
        return carry

    lax.fori_loop(0, c_all, take, 0)
    stats[2, hd] = jnp.zeros((16, 128), F32)
    for p in range(2):
        for i in range(na):
            cut = slice(i * la, (i + 1) * la)
            raw = araw[p, i * la // tok : (i + 1) * la // tok].reshape(la, f).astype(F32)
            term = raw * ag[p : p + 1] * aun[p, cut].astype(F32)
            at = 2 * nv + p * na + i
            stats[2, hd, at : at + 1] = to_row(jnp.sum(term, 1, keepdims=True))
    share(2)
    ga[2] = aun[2].reshape(n, tok, f)
    oa[...] = aun[3].reshape(n, tok, f)
    inner[...] = rates[...] * rates[...] * rates[...] * shared(2) / feat_all
    for p in range(2):
        for i in range(na):
            cut = slice(i * la, (i + 1) * la)
            owned = slice(i * la // tok, (i + 1) * la // tok)
            at = 2 * nv + p * na + i
            raw = araw[p, owned].reshape(la, f).astype(F32)
            back = (
                ag[p : p + 1] * aun[p, cut].astype(F32) * to_column(rates[at : at + 1], la)
                - raw * to_column(inner[at : at + 1], la)
            )
            ga[p, owned] = back.astype(BF16).reshape(la // tok, tok, f)

    for kind in range(2):
        for copy in video_halo(kind):
            copy.wait_send()

    def drain(c, carry):
        sent(msg, a2a_send, c)
        sent(ret, ret_send, c)
        for copy in audio_halo(c) + grad_halo(evs, evr, ev_send, ev_recv, c) + grad_halo(eas, ear, ea_send, ea_recv, c):
            copy.wait_send()
        return carry

    lax.fori_loop(0, c_all, drain, 0)
    put_ov.wait()
    put_gv.wait()


def local(video_qkv, audio_qkv, video_gain, audio_gain, video_cot, audio_cot, intersection, lengths):
    n, x = lax.axis_size("tm"), lax.axis_size("head")
    f = video_qkv.shape[2]
    v_rows, a_rows = video_qkv.shape[1], n * audio_qkv.shape[2]
    ga_rows = a_rows // VB
    ae_rows, ve_rows = a_rows + 2 * ga_rows, v_rows + 2 * VBLK
    hbm = pl.BlockSpec(memory_space=pltpu.HBM)
    vmem = pl.BlockSpec(memory_space=pltpu.VMEM)
    dma = pltpu.SemaphoreType.DMA
    bf = lambda *shape: pltpu.VMEM(shape, BF16)
    f32 = lambda *shape: pltpu.VMEM(shape, F32)
    scratch = [
        bf(2, v_rows, f), bf(v_rows, f), bf(3, n, 4, f), bf(n, 4, f),
        bf(v_rows, f), bf(2, ve_rows, f), bf(n, 16, f), bf(n, 16, f),
        bf(a_rows, f), bf(2, ae_rows, f), bf(a_rows, f),
        bf(v_rows, f), f32(v_rows, f), f32(2, v_rows, f),
        bf(a_rows, f), f32(2, ae_rows, f), bf(a_rows, f),
        bf(2, 2, VBLK, f), bf(2, 2, VBLK, f), bf(2, 2, ga_rows, f), bf(2, 2, ga_rows, f),
        bf(n, 16, f), bf(n, 16, f), bf(4, a_rows, f), bf(3, v_rows, f),
        f32(VB, 3 * ga_rows, VBLK), f32(2, 4 * VBLK, 2 * ga_rows), f32(a_rows, 128),
        f32(3, x, 16, 128), f32(16, 128), f32(16, 128),
        dma((5,)), dma((2,)), dma((3,)), dma((3,)), dma((2, 2)), dma((2, 2)),
        dma((CHUNKS, 2)), dma((CHUNKS, 2)), dma((CHUNKS,)), dma((CHUNKS,)),
        dma((CHUNKS, 2)), dma((CHUNKS, 2)), dma((CHUNKS, 2)), dma((CHUNKS, 2)),
        dma((CHUNKS,)), dma((CHUNKS,)),
    ]
    out_video, out_audio, grad_video, grad_audio = pl.pallas_call(
        functools.partial(kernel, (n, x, f)),
        out_shape=(
            jax.ShapeDtypeStruct(video_cot.shape, BF16),
            jax.ShapeDtypeStruct(audio_cot.shape, BF16),
            jax.ShapeDtypeStruct(video_qkv.shape, BF16),
            jax.ShapeDtypeStruct(audio_qkv.shape, BF16),
        ),
        in_specs=[hbm, hbm, vmem, vmem, hbm, hbm, vmem, vmem],
        out_specs=(hbm, vmem, hbm, vmem),
        scratch_shapes=scratch,
        compiler_params=pltpu.CompilerParams(
            collective_id=0, has_side_effects=True, vmem_limit_bytes=56 << 20
        ),
        name="window",
    )(
        video_qkv, audio_qkv, video_gain, audio_gain, video_cot, audio_cot,
        intersection.T, lengths[None],
    )
    return out_video, out_audio, grad_video, grad_audio


def solution(mesh):
    return jax.shard_map(
        local,
        mesh=mesh,
        in_specs=(
            P(None, "tm", "head"),
            P(None, None, "tm", "head"),
            P(None, "head"),
            P(None, "head"),
            P("tm", "head"),
            P(None, "tm", "head"),
            P(),
            P(),
        ),
        out_specs=(
            P("tm", "head"),
            P(None, "tm", "head"),
            P(None, "tm", "head"),
            P(None, None, "tm", "head"),
        ),
        check_vma=False,
    )
```

time: 293 us -> 122 us (0.42)
  the two profiles are of different devices: /device:TPU:34 before, /device:TPU:1 now
where the time goes in v1:
time: 122 us; the launch traced here: 121 us
  Pallas kernels  114 us (93%)
  local copies, waits for them, and re-layouts  7.21 us (6%)
    pallas_call x1, Pallas kernels, local(): pl.pallas_call(functools.partial(kernel, (n, x, f)), out_shape=(jax.Shape...  114 us
    unnamed x8, local copies, waits for them, and re-layouts  7.21 us

profile of v1, /device:TPU:1, one launch (start us, length us, event | category | flops | bytes accessed | tf_op | source)
XLA Modules:
  0.0 121.4 jit_solution(16917793694143379403)
XLA Ops:
  0.6 113.5 %window.1 = (bf16[512,768]{1,0:T(8,128)(2,1)}, bf16[64,4,768]{2,1,0:T(4,128)(2,1)}, bf16[3,512,768]{2,1,0:T(8,128)(2,1)}, bf16[3,64,4,768]{3,2,1,0:T(4,128)(2,1)}) custom-call(bf16[3,512,768]{2,1,0:T(8,128)(2,1)} %vq_hbm.1, bf16[3,64,4,768]{3,2,1,0:T(4,128)(2,1)} %aq_hbm.1, f32[2,768]{1,0:T(2,128)} %vg.1, f32[2,768]{1,0:T(2,128)} %ag.1, ...), custom_call_target="tpu_custom_call" | custom-call | tf_op jit(solution)/shard_map/window/pallas_call | solution.py:502
  114.2 0.0 copy-start
  114.2 2.2 %copy.16 = bf16[512,768]{1,0:T(8,128)(2,1)} copy(bf16[512,768]{1,0:T(8,128)(2,1)} %get-tuple-element.8) | data formatting | bytes 1572864
  116.4 1.9 %copy.17 = bf16[64,4,768]{2,1,0:T(4,128)(2,1)} copy(bf16[64,4,768]{2,1,0:T(4,128)(2,1)} %get-tuple-element.9) | data formatting | bytes 786432
  118.3 0.0 copy-done
  118.3 0.0 copy-start.1
  118.3 1.4 %copy.18 = bf16[3,512,768]{2,1,0:T(8,128)(2,1)} copy(bf16[3,512,768]{2,1,0:T(8,128)(2,1)S(1)} %copy-done) | data formatting | bytes 4718592
  119.7 0.7 copy-done.1
  120.4 1.0 copy.19
Async XLA Ops:
  114.2 4.1 %copy-start = (bf16[3,512,768]{2,1,0:T(8,128)(2,1)S(1)}, bf16[3,512,768]{2,1,0:T(8,128)(2,1)}, u32[]{:S(2)}) copy-start(bf16[3,512,768]{2,1,0:T(8,128)(2,1)} %get-tuple-element.10) | copy-start | bytes 7077892
  118.3 2.1 %copy-start.1 = (bf16[3,64,4,768]{3,2,1,0:T(4,128)(2,1)S(1)}, bf16[3,64,4,768]{3,2,1,0:T(4,128)(2,1)}, u32[]{:S(2)}) copy-start(bf16[3,64,4,768]{3,2,1,0:T(4,128)(2,1)} %get-tuple-element.11) | copy-start | bytes 3538948

commit v2 on v1

--- a/solution.py
+++ b/solution.py
@@ -56,12 +56,12 @@
 
 def kernel(
     dims,
-    vq_hbm, aq_hbm, vg, ag, vc_hbm, ac_hbm, inter, lens,
-    ov_hbm, oa, gv_hbm, ga,
-    vraw, vcot, araw, acot, vqn, vkv, msg, win, aqn, akv, acw,
-    ov, dqv, dvkv, dqa, dakv, oaw, evs, evr, eas, ear, ret, retr, aun, gv,
+    vq_hbm, aq_hbm, vg_hbm, ag_hbm, vc_hbm, ac_hbm, inter_hbm, lens_hbm,
+    ov, oa, gv, ga,
+    vg, ag, inter, lens, vraw, vcot, araw, acot, vqn, vkv, msg, win, aqn, akv, acw,
+    dqv, dvkv, dqa, dakv, oaw, evs, evr, eas, ear, ret, retr, aun,
     vab, avb, live, stats, rates, inner,
-    in_sem, out_sem, st_send, st_recv, vh_send, vh_recv, ah_send, ah_recv,
+    in_sem, st_send, st_recv, vh_send, vh_recv, ah_send, ah_recv,
     a2a_send, a2a_recv, ev_send, ev_recv, ea_send, ea_recv, ret_send, ret_recv,
 ):
     n, x, f = dims
@@ -95,6 +95,10 @@
         pltpu.make_async_copy(ac_hbm, acot, in_sem.at[2]),
         pltpu.make_async_copy(vq_hbm.at[2], vkv.at[1, pl.ds(VBLK, v_rows)], in_sem.at[3]),
         pltpu.make_async_copy(vc_hbm, vcot, in_sem.at[4]),
+        pltpu.make_async_copy(inter_hbm, inter, in_sem.at[5]),
+        pltpu.make_async_copy(lens_hbm, lens, in_sem.at[6]),
+        pltpu.make_async_copy(vg_hbm, vg, in_sem.at[7]),
+        pltpu.make_async_copy(ag_hbm, ag, in_sem.at[8]),
     ]
     for load in loads:
         load.start()
@@ -108,6 +112,8 @@
     block = start + lax.shift_right_logical(rows, 2)
     block = jnp.where(block < 0, block + blocks, block)
     block = jnp.where(block >= blocks, block - blocks, block)
+    loads[5].wait()
+    loads[6].wait()
     tables = []
     for ref, at in ((inter, 0), (inter, 1), (lens, 0)):
         column = jnp.zeros((ae_rows, 1), F32)
@@ -153,9 +159,8 @@
             raw = vraw[p, i * lv : (i + 1) * lv].astype(F32)
             at = p * nv + i
             stats[0, hd, at : at + 1] = to_row(jnp.sum(raw * raw, 1, keepdims=True))
-    loads[2].wait()
-    loads[3].wait()
-    loads[4].wait()
+    for i in (2, 3, 4, 7, 8):
+        loads[i].wait()
 
     def share(turn):
         copies = []
@@ -184,6 +189,30 @@
             src, dst, send, recv, device_id={"tm": to}, device_id_type=MESH
         )
 
+    size = 4 * ga_rows
+    one, two = iota((size, size), 0), iota((size, size), 1)
+
+    def moved(row):
+        arr = lax.rem(lax.div(row, tok), 4)
+        return arr * ga_rows + lax.div(row, 4 * tok) * tok + lax.rem(row, tok)
+
+    pack = jnp.where(two == moved(one), 1.0, 0.0).astype(BF16)
+    unpack = jnp.where(one == moved(two), 1.0, 0.0).astype(BF16)
+
+    def lane(c, h):
+        return slice(c * w + h * HD, c * w + (h + 1) * HD)
+
+    def put_messages(dst, kind, c, j, arrays):
+        parts = [array[:, lane(c, h)] for h in range(heads) for array in arrays]
+        packed = mm(pack, jnp.concatenate(parts, 0), 1, 0).astype(BF16)
+        dst[kind, c, j * nb : (j + 1) * nb] = packed.reshape(nb, 16, HD)
+
+    for j in range(VB):
+        cut = slice(j * nb, (j + 1) * nb)
+        arrays = araw[2, cut].reshape(ga_rows, f), acot[cut].reshape(ga_rows, f)
+        for c in range(c_all):
+            put_messages(msg, 0, c, j, arrays)
+
     pl.semaphore_wait(barrier, n - 1 + x - 1)
     share(0)
 
@@ -197,62 +226,47 @@
 
     for copy in video_halo(1):
         copy.start()
+
+    def lanes_of(c):
+        return pl.ds(pl.multiple_of(c * w, w), w)
+
+    def spread(src, dst, send, recv):
+        def chunk(kind, c):
+            def one_device(k, carry):
+                d = lax.rem(me + k, n)
+                edge_copy(src.at[kind, c, d], dst.at[kind, c, me], send.at[kind, c], recv.at[kind, c], d).start()
+                return carry
+
+            lax.fori_loop(1, n, one_device, 0)
+            pltpu.make_async_copy(src.at[kind, c, me], dst.at[kind, c, me], recv.at[kind, c]).start()
+
+        return chunk
+
+    def landed(dst, recv, kind, c):
+        some = dst.at[kind, c]
+        pltpu.make_async_copy(some, some, recv.at[kind, c]).wait()
+
+    def sent(src, send, kind, c):
+        some = src.at[kind, c, pl.ds(0, n - 1)]
+        pltpu.make_async_copy(some, some, send.at[kind, c]).wait()
+
+    spread_out = spread(msg, win, a2a_send, a2a_recv)
+    spread_back = spread(ret, retr, ret_send, ret_recv)
+
+    def each_chunk(fn):
+        def body(c, carry):
+            fn(c)
+            return carry
+
+        lax.fori_loop(0, c_all, body, 0)
+
+    each_chunk(lambda c: spread_out(0, c))
     rates[...] = lax.rsqrt(shared(0) / feat_all + EPSILON)
-
-    size = 4 * ga_rows
-    one, two = iota((size, size), 0), iota((size, size), 1)
-
-    def moved(row):
-        arr = lax.rem(lax.div(row, tok), 4)
-        return arr * ga_rows + lax.div(row, 4 * tok) * tok + lax.rem(row, tok)
-
-    pack = jnp.where(two == moved(one), 1.0, 0.0).astype(BF16)
-    unpack = jnp.where(one == moved(two), 1.0, 0.0).astype(BF16)
 
     def audio_rate(p, row_at, row_count):
         i, off = divmod(row_at, la)
         at = 2 * nv + p * na + i
         return to_column(rates[at : at + 1], la)[off : off + row_count]
-
-    for j in range(VB):
-        cut = slice(j * nb, (j + 1) * nb)
-        parts = []
-        for p in range(2):
-            raw = araw[p, cut].reshape(ga_rows, f).astype(F32)
-            normed = raw * audio_rate(p, j * ga_rows, ga_rows) * ag[p : p + 1]
-            parts.append(normed.astype(BF16))
-        parts.append(araw[2, cut].reshape(ga_rows, f))
-        parts.append(acot[cut].reshape(ga_rows, f))
-        packed = mm(pack, jnp.concatenate(parts, 0), 1, 0).astype(BF16)
-        msg[cut] = packed.reshape(nb, 16, f)
-
-    def lanes_of(c):
-        return pl.ds(pl.multiple_of(c * w, w), w)
-
-    def spread(src, dst, send, recv):
-        def chunk(c, carry):
-            lanes = lanes_of(c)
-
-            def one_device(k, inner_carry):
-                d = lax.rem(me + k, n)
-                edge_copy(src.at[d, :, lanes], dst.at[me, :, lanes], send.at[c], recv.at[c], d).start()
-                return inner_carry
-
-            lax.fori_loop(1, n, one_device, 0)
-            pltpu.make_async_copy(src.at[me, :, lanes], dst.at[me, :, lanes], recv.at[c]).start()
-            return carry
-
-        return chunk
-
-    def landed(dst, recv, c):
-        some = dst.at[:, :, lanes_of(c)]
-        pltpu.make_async_copy(some, some, recv.at[c]).wait()
-
-    def sent(src, send, c):
-        some = src.at[pl.ds(0, n - 1), :, lanes_of(c)]
-        pltpu.make_async_copy(some, some, send.at[c]).wait()
-
-    lax.fori_loop(0, c_all, spread(msg, win, a2a_send, a2a_recv), 0)
 
     for p in (1, 0):
         for i in range(nv):
@@ -268,15 +282,26 @@
             for copy in video_halo(0):
                 copy.start()
 
-    def audio_halo(c):
+    for j in range(VB):
+        cut = slice(j * nb, (j + 1) * nb)
+        arrays = []
+        for p in range(2):
+            raw = araw[p, cut].reshape(ga_rows, f).astype(F32)
+            normed = raw * audio_rate(p, j * ga_rows, ga_rows) * ag[p : p + 1]
+            arrays.append(normed.astype(BF16))
+        for c in range(c_all):
+            put_messages(msg, 1, c, j, arrays)
+    each_chunk(lambda c: spread_out(1, c))
+
+    def audio_halo(kind, c):
         lanes = lanes_of(c)
         return (
-            edge_copy(akv.at[:, pl.ds(ga_rows, ga_rows), lanes],
-                      akv.at[:, pl.ds(ga_rows + a_rows, ga_rows), lanes],
-                      ah_send.at[c, 0], ah_recv.at[c, 0], left),
-            edge_copy(akv.at[:, pl.ds(a_rows, ga_rows), lanes],
-                      akv.at[:, pl.ds(0, ga_rows), lanes],
-                      ah_send.at[c, 1], ah_recv.at[c, 1], right),
+            edge_copy(akv.at[kind, pl.ds(ga_rows, ga_rows), lanes],
+                      akv.at[kind, pl.ds(ga_rows + a_rows, ga_rows), lanes],
+                      ah_send.at[kind, c, 0], ah_recv.at[kind, c, 0], left),
+            edge_copy(akv.at[kind, pl.ds(a_rows, ga_rows), lanes],
+                      akv.at[kind, pl.ds(0, ga_rows), lanes],
+                      ah_send.at[kind, c, 1], ah_recv.at[kind, c, 1], right),
         )
 
     def grad_halo(src, dst, send, recv, c):
@@ -286,50 +311,72 @@
             edge_copy(src.at[1, :, :, lanes], dst.at[0, :, :, lanes], send.at[c, 1], recv.at[c, 1], right),
         )
 
-    spread_back = spread(ret, retr, ret_send, ret_recv)
+    def lane_at(c, h):
+        return pl.ds(pl.multiple_of(c * w + h * HD, HD), HD)
 
     def finish(c):
-        lanes = lanes_of(c)
         for copy in grad_halo(eas, ear, ea_send, ea_recv, c):
             copy.wait_recv()
         for j in range(VB):
             cut = slice(j * ga_rows, (j + 1) * ga_rows)
-            parts = [dqa[cut, lanes]]
+            ext = slice((j + 1) * ga_rows, (j + 2) * ga_rows)
+            parts = [], []
+            for h in range(heads):
+                at = lane_at(c, h)
+                grads = []
+                for kind in range(2):
+                    total = dakv[kind, ext, at]
+                    if j == 0:
+                        total = total + ear[0, kind, :, at].astype(F32)
+                    if j == VB - 1:
+                        total = total + ear[1, kind, :, at].astype(F32)
+                    grads.append(total.astype(BF16))
+                parts[0].extend((oaw[cut, at], grads[1]))
+                parts[1].extend((dqa[cut, at], grads[0]))
             for kind in range(2):
-                total = dakv[kind, (j + 1) * ga_rows : (j + 2) * ga_rows, lanes]
-                if j == 0:
-                    total = total + ear[0, kind, :, lanes].astype(F32)
-                if j == VB - 1:
-                    total = total + ear[1, kind, :, lanes].astype(F32)
-                parts.append(total.astype(BF16))
-            parts.append(oaw[cut, lanes])
-            packed = mm(pack, jnp.concatenate(parts, 0), 1, 0).astype(BF16)
-            ret[j * nb : (j + 1) * nb, :, lanes] = packed.reshape(nb, 16, w)
-        spread_back(c, 0)
-
-    def chunk_work(c, carry):
-        lanes = lanes_of(c)
-        landed(win, a2a_recv, c)
+                packed = mm(pack, jnp.concatenate(parts[kind], 0), 1, 0).astype(BF16)
+                ret[kind, c, j * nb : (j + 1) * nb] = packed.reshape(nb, 16, HD)
+
+    def unpacked(src, kind, c, j):
+        rows = src[kind, c, j * nb : (j + 1) * nb].reshape(size, HD)
+        return mm(unpack, rows, 1, 0)
+
+    def take_values(c):
+        landed(win, a2a_recv, 0, c)
         for j in range(VB):
-            some = win[j * nb : (j + 1) * nb, :, lanes].reshape(size, w)
-            some = mm(unpack, some, 1, 0)
+            some = unpacked(win, 0, c, j)
             cut = slice(j * ga_rows, (j + 1) * ga_rows)
             ext = slice((j + 1) * ga_rows, (j + 2) * ga_rows)
-            aqn[cut, lanes] = some[:ga_rows].astype(BF16)
-            akv[0, ext, lanes] = some[ga_rows : 2 * ga_rows].astype(BF16)
-            akv[1, ext, lanes] = some[2 * ga_rows : 3 * ga_rows].astype(BF16)
-            acw[cut, lanes] = jnp.where(live[cut, :1] > 0.0, some[3 * ga_rows :], 0.0).astype(BF16)
-        for copy in audio_halo(c):
+            for h in range(heads):
+                at = lane_at(c, h)
+                top = 2 * h * ga_rows
+                akv[1, ext, at] = some[top : top + ga_rows].astype(BF16)
+                cots = some[top + ga_rows : top + 2 * ga_rows]
+                acw[cut, at] = jnp.where(live[cut, :1] > 0.0, cots, 0.0).astype(BF16)
+        for copy in audio_halo(1, c):
             copy.start()
 
-        @pl.when(c == 0)
-        def _():
-            for kind in range(2):
-                for copy in video_halo(kind):
-                    copy.wait_recv()
+    each_chunk(take_values)
+    for kind in range(2):
+        for copy in video_halo(kind):
+            copy.wait_recv()
+
+    def chunk_work(c):
+        landed(win, a2a_recv, 1, c)
+        for j in range(VB):
+            some = unpacked(win, 1, c, j)
+            cut = slice(j * ga_rows, (j + 1) * ga_rows)
+            ext = slice((j + 1) * ga_rows, (j + 2) * ga_rows)
+            for h in range(heads):
+                at = lane_at(c, h)
+                top = 2 * h * ga_rows
+                aqn[cut, at] = some[top : top + ga_rows].astype(BF16)
+                akv[0, ext, at] = some[top + ga_rows : top + 2 * ga_rows].astype(BF16)
+        for copy in audio_halo(0, c):
+            copy.start()
 
         for h in range(heads):
-            at = pl.ds(pl.multiple_of(c * w + h * HD, HD), HD)
+            at = lane_at(c, h)
             sums = [[None] * 6, [None] * 6]
             for p in range(2):
                 cut = slice(p * pair, (p + 1) * pair)
@@ -351,10 +398,21 @@
                     dvkv[kind, e * VBLK : (e + 1) * VBLK, at] = sums[kind][e + 1]
         for copy in grad_halo(evs, evr, ev_send, ev_recv, c):
             copy.start()
-        for copy in audio_halo(c):
-            copy.wait_recv()
+
+        @pl.when(c > 0)
+        def _():
+            finish(c - 1)
+            spread_back(1, c - 1)
+
+        @pl.when(c == 1)
+        def _():
+            spread_back(0, 0)
+
+        for kind in range(2):
+            for copy in audio_halo(kind, c):
+                copy.wait_recv()
         for h in range(heads):
-            at = pl.ds(pl.multiple_of(c * w + h * HD, HD), HD)
+            at = lane_at(c, h)
             sums = [[None] * 6, [None] * 6]
             for b in range(VB):
                 cut = slice(b * VBLK, (b + 1) * VBLK)
@@ -377,23 +435,17 @@
         for copy in grad_halo(eas, ear, ea_send, ea_recv, c):
             copy.start()
 
-        @pl.when(c > 0)
-        def _():
-            finish(c - 1)
-
-        return carry
-
-    lax.fori_loop(0, c_all, chunk_work, 0)
-    put_ov = pltpu.make_async_copy(ov, ov_hbm, out_sem.at[0])
-    put_ov.start()
+    each_chunk(chunk_work)
     finish(c_all - 1)
-
-    def wait_edges(c, carry):
+    spread_back(1, c_all - 1)
+    for c in range(1, c_all):
+        spread_back(0, c)
+
+    def wait_edges(c):
         for copy in grad_halo(evs, evr, ev_send, ev_recv, c):
             copy.wait_recv()
-        return carry
-
-    lax.fori_loop(0, c_all, wait_edges, 0)
+
+    each_chunk(wait_edges)
     for kind in range(2):
         head_rows, tail_rows = slice(0, VBLK), slice(v_rows - VBLK, v_rows)
         dvkv[kind, head_rows] = dvkv[kind, head_rows] + evr[0, kind].astype(F32)
@@ -419,20 +471,18 @@
             rate = to_column(rates[at : at + 1], lv)
             back = vg[p : p + 1] * grad * rate - vraw[p, cut].astype(F32) * to_column(inner[at : at + 1], lv)
             gv[p, cut] = back.astype(BF16)
-    put_gv = pltpu.make_async_copy(gv, gv_hbm, out_sem.at[1])
-    put_gv.start()
-
-    def take(c, carry):
-        lanes = lanes_of(c)
-        landed(retr, ret_recv, c)
+
+    def take_grads(c):
+        landed(retr, ret_recv, 1, c)
         for j in range(VB):
-            some = retr[j * nb : (j + 1) * nb, :, lanes].reshape(size, w)
-            some = mm(unpack, some, 1, 0).astype(BF16)
-            for arr in range(4):
-                aun[arr, j * ga_rows : (j + 1) * ga_rows, lanes] = some[arr * ga_rows : (arr + 1) * ga_rows]
-        return carry
-
-    lax.fori_loop(0, c_all, take, 0)
+            some = unpacked(retr, 1, c, j).astype(BF16)
+            cut = slice(j * ga_rows, (j + 1) * ga_rows)
+            for h in range(heads):
+                for arr in range(2):
+                    top = (2 * h + arr) * ga_rows
+                    aun[arr, cut, lane_at(c, h)] = some[top : top + ga_rows]
+
+    each_chunk(take_grads)
     stats[2, hd] = jnp.zeros((16, 128), F32)
     for p in range(2):
         for i in range(na):
@@ -442,8 +492,6 @@
             at = 2 * nv + p * na + i
             stats[2, hd, at : at + 1] = to_row(jnp.sum(term, 1, keepdims=True))
     share(2)
-    ga[2] = aun[2].reshape(n, tok, f)
-    oa[...] = aun[3].reshape(n, tok, f)
     inner[...] = rates[...] * rates[...] * rates[...] * shared(2) / feat_all
     for p in range(2):
         for i in range(na):
@@ -457,20 +505,50 @@
             )
             ga[p, owned] = back.astype(BF16).reshape(la // tok, tok, f)
 
+    def take_outputs(c):
+        landed(retr, ret_recv, 0, c)
+        for j in range(VB):
+            some = unpacked(retr, 0, c, j).astype(BF16)
+            cut = slice(j * nb, (j + 1) * nb)
+            for h in range(heads):
+                top = 2 * h * ga_rows
+                at = lane_at(c, h)
+                oa[cut, :, at] = some[top : top + ga_rows].reshape(nb, tok, HD)
+                ga[2, cut, :, at] = some[top + ga_rows : top + 2 * ga_rows].reshape(nb, tok, HD)
+
+    each_chunk(take_outputs)
+
     for kind in range(2):
         for copy in video_halo(kind):
             copy.wait_send()
 
-    def drain(c, carry):
-        sent(msg, a2a_send, c)
-        sent(ret, ret_send, c)
-        for copy in audio_halo(c) + grad_halo(evs, evr, ev_send, ev_recv, c) + grad_halo(eas, ear, ea_send, ea_recv, c):
+    def drain(c):
+        edges = grad_halo(evs, evr, ev_send, ev_recv, c) + grad_halo(eas, ear, ea_send, ea_recv, c)
+        for kind in range(2):
+            sent(msg, a2a_send, kind, c)
+            sent(ret, ret_send, kind, c)
+            edges = edges + audio_halo(kind, c)
+        for copy in edges:
             copy.wait_send()
-        return carry
-
-    lax.fori_loop(0, c_all, drain, 0)
-    put_ov.wait()
-    put_gv.wait()
+
+    each_chunk(drain)
+
+
+def store(ov, oa, gv, ga, ov_out, oa_out, gv_out, ga_out, sem):
+    half = ov.shape[0] // 2
+    pairs = [(oa, oa_out)]
+    for i in range(2):
+        rows = pl.ds(i * half, half)
+        pairs += [(gv.at[p, rows], gv_out.at[p, rows]) for p in range(3)]
+        pairs.append((ov.at[rows], ov_out.at[rows]))
+    pairs += [(ga.at[p], ga_out.at[p]) for p in range(3)]
+    copies = [
+        pltpu.make_async_copy(src, dst, sem.at[i // 8, i % 8]) for i, (src, dst) in enumerate(pairs)
+    ]
+    for copy in copies:
+        copy.start()
+    for copy in copies:
+        copy.wait()
 
 
 def local(video_qkv, audio_qkv, video_gain, audio_gain, video_cot, audio_cot, intersection, lengths):
@@ -485,21 +563,23 @@
     bf = lambda *shape: pltpu.VMEM(shape, BF16)
     f32 = lambda *shape: pltpu.VMEM(shape, F32)
     scratch = [
+        f32(2, f), f32(2, f), pltpu.VMEM((2, n * n), jnp.int32), pltpu.VMEM((1, n * n), jnp.int32),
         bf(2, v_rows, f), bf(v_rows, f), bf(3, n, 4, f), bf(n, 4, f),
-        bf(v_rows, f), bf(2, ve_rows, f), bf(n, 16, f), bf(n, 16, f),
+        bf(v_rows, f), bf(2, ve_rows, f), bf(2, CHUNKS, n, 16, HD), bf(2, CHUNKS, n, 16, HD),
         bf(a_rows, f), bf(2, ae_rows, f), bf(a_rows, f),
-        bf(v_rows, f), f32(v_rows, f), f32(2, v_rows, f),
+        f32(v_rows, f), f32(2, v_rows, f),
         bf(a_rows, f), f32(2, ae_rows, f), bf(a_rows, f),
         bf(2, 2, VBLK, f), bf(2, 2, VBLK, f), bf(2, 2, ga_rows, f), bf(2, 2, ga_rows, f),
-        bf(n, 16, f), bf(n, 16, f), bf(4, a_rows, f), bf(3, v_rows, f),
+        bf(2, CHUNKS, n, 16, HD), bf(2, CHUNKS, n, 16, HD), bf(2, a_rows, f),
         f32(VB, 3 * ga_rows, VBLK), f32(2, 4 * VBLK, 2 * ga_rows), f32(a_rows, 128),
         f32(3, x, 16, 128), f32(16, 128), f32(16, 128),
-        dma((5,)), dma((2,)), dma((3,)), dma((3,)), dma((2, 2)), dma((2, 2)),
-        dma((CHUNKS, 2)), dma((CHUNKS, 2)), dma((CHUNKS,)), dma((CHUNKS,)),
+        dma((9,)), dma((3,)), dma((3,)), dma((2, 2)), dma((2, 2)),
+        dma((2, CHUNKS, 2)), dma((2, CHUNKS, 2)), dma((2, CHUNKS)), dma((2, CHUNKS)),
         dma((CHUNKS, 2)), dma((CHUNKS, 2)), dma((CHUNKS, 2)), dma((CHUNKS, 2)),
-        dma((CHUNKS,)), dma((CHUNKS,)),
+        dma((2, CHUNKS)), dma((2, CHUNKS)),
     ]
-    out_video, out_audio, grad_video, grad_audio = pl.pallas_call(
+    stay = lambda array: pltpu.with_memory_space_constraint(array, pltpu.HBM)
+    results = pl.pallas_call(
         functools.partial(kernel, (n, x, f)),
         out_shape=(
             jax.ShapeDtypeStruct(video_cot.shape, BF16),
@@ -507,18 +587,26 @@
             jax.ShapeDtypeStruct(video_qkv.shape, BF16),
             jax.ShapeDtypeStruct(audio_qkv.shape, BF16),
         ),
-        in_specs=[hbm, hbm, vmem, vmem, hbm, hbm, vmem, vmem],
-        out_specs=(hbm, vmem, hbm, vmem),
+        in_specs=[hbm] * 8,
+        out_specs=(vmem, vmem, vmem, vmem),
         scratch_shapes=scratch,
         compiler_params=pltpu.CompilerParams(
-            collective_id=0, has_side_effects=True, vmem_limit_bytes=56 << 20
+            collective_id=0, has_side_effects=True, vmem_limit_bytes=40 << 20
         ),
         name="window",
     )(
-        video_qkv, audio_qkv, video_gain, audio_gain, video_cot, audio_cot,
-        intersection.T, lengths[None],
+        *map(stay, (video_qkv, audio_qkv, video_gain, audio_gain, video_cot, audio_cot)),
+        stay(intersection.T), stay(lengths[None]),
     )
-    return out_video, out_audio, grad_video, grad_audio
+    return pl.pallas_call(
+        store,
+        out_shape=tuple(jax.ShapeDtypeStruct(result.shape, BF16) for result in results),
+        in_specs=[vmem] * 4,
+        out_specs=(hbm,) * 4,
+        scratch_shapes=[dma((2, 8))],
+        compiler_params=pltpu.CompilerParams(vmem_limit_bytes=16 << 20),
+        name="store",
+    )(*results)
 
 
 def solution(mesh):

time: 122 us -> 109 us (0.89)
  local copies, waits for them, and re-layouts: 7.21 us -> 0 us
  Pallas kernels: 114 us -> 108 us
    pallas_call x1, Pallas kernels: 114 us -> 106 us  [local(): pl.pallas_call(functools.partial(kernel, (n, x, f)), out_shape=(jax.Shape...]
    unnamed x8 -> x0, local copies, waits for them, and re-layouts: 7.21 us -> none
    pallas_call x0 -> x1, Pallas kernels: none -> 2.31 us  [local(): pl.pallas_call(store, out_shape=tuple((jax.ShapeDtypeStruct(result.shape,...]
where the time goes in v2:
time: 109 us; the launch traced here: 108 us
  Pallas kernels  108 us (99%)
    pallas_call x1, Pallas kernels, local(): pl.pallas_call(functools.partial(kernel, (n, x, f)), out_shape=(jax.Shape...  106 us
    pallas_call x1, Pallas kernels, local(): pl.pallas_call(store, out_shape=tuple((jax.ShapeDtypeStruct(result.shape,...  2.31 us

profile of v2, /device:TPU:1, one launch (start us, length us, event | category | flops | bytes accessed | tf_op | source)
XLA Modules:
  0.0 108.5 jit_solution(3054143166031436434)
XLA Ops:
  0.6 105.5 %window.1 = (bf16[512,768]{1,0:T(8,128)(2,1)S(1)}, bf16[64,4,768]{2,1,0:T(4,128)(2,1)S(1)}, bf16[3,512,768]{2,1,0:T(8,128)(2,1)S(1)}, bf16[3,64,4,768]{3,2,1,0:T(4,128)(2,1)S(1)}) custom-call(bf16[3,512,768]{2,1,0:T(8,128)(2,1)} %vq_hbm.1, bf16[3,64,4,768]{3,2,1,0:T(4,128)(2,1)} %aq_hbm.1, f32[2,768]{1,0:T(2,128)} %vg_hbm.1, f32[2,768]{1,0:T(2,128)} %ag_hbm.1, ...), custom_call_target="tpu_custom_call" | custom-call | tf_op jit(solution)/shard_map/window/pallas_call | solution.py:582
  106.2 2.3 %store.1 = (bf16[512,768]{1,0:T(8,128)(2,1)}, bf16[64,4,768]{2,1,0:T(4,128)(2,1)}, bf16[3,512,768]{2,1,0:T(8,128)(2,1)}, bf16[3,64,4,768]{3,2,1,0:T(4,128)(2,1)}) custom-call(bf16[512,768]{1,0:T(8,128)(2,1)S(1)} %get-tuple-element.8.ov, bf16[64,4,768]{2,1,0:T(4,128)(2,1)S(1)} %get-tuple-element.9.oa, bf16[3,512,768]{2,1,0:T(8,128)(2,1)S(1)} %get-tuple-element.10.gv, ...), custom_call_target="tpu_custom_call" | custom-call | tf_op jit(solution)/shard_map/store/pallas_call | solution.py:601

commit v3 on v2

--- a/solution.py
+++ b/solution.py
@@ -260,7 +260,7 @@
 
         lax.fori_loop(0, c_all, body, 0)
 
-    each_chunk(lambda c: spread_out(0, c))
+    spread_out(0, 0)
     rates[...] = lax.rsqrt(shared(0) / feat_all + EPSILON)
 
     def audio_rate(p, row_at, row_count):
@@ -291,7 +291,7 @@
             arrays.append(normed.astype(BF16))
         for c in range(c_all):
             put_messages(msg, 1, c, j, arrays)
-    each_chunk(lambda c: spread_out(1, c))
+    spread_out(1, 0)
 
     def audio_halo(kind, c):
         lanes = lanes_of(c)
@@ -356,7 +356,8 @@
         for copy in audio_halo(1, c):
             copy.start()
 
-    each_chunk(take_values)
+    take_values(0)
+    spread_out(0, 1)
     for kind in range(2):
         for copy in video_halo(kind):
             copy.wait_recv()
@@ -374,6 +375,14 @@
                 akv[0, ext, at] = some[top + ga_rows : top + 2 * ga_rows].astype(BF16)
         for copy in audio_halo(0, c):
             copy.start()
+
+        @pl.when(c < c_all - 1)
+        def _():
+            spread_out(1, c + 1)
+
+        @pl.when(c == c_all - 1)
+        def _():
+            spread_back(0, 0)
 
         for h in range(heads):
             at = lane_at(c, h)
@@ -402,11 +411,10 @@
         @pl.when(c > 0)
         def _():
             finish(c - 1)
-            spread_back(1, c - 1)
 
         @pl.when(c == 1)
         def _():
-            spread_back(0, 0)
+            spread_back(1, 0)
 
         for kind in range(2):
             for copy in audio_halo(kind, c):
@@ -435,7 +443,16 @@
         for copy in grad_halo(eas, ear, ea_send, ea_recv, c):
             copy.start()
 
+        @pl.when(c < c_all - 1)
+        def _():
+            take_values(c + 1)
+
+        @pl.when(c < c_all - 2)
+        def _():
+            spread_out(0, c + 2)
+
     each_chunk(chunk_work)
+    spread_back(1, c_all - 2)
     finish(c_all - 1)
     spread_back(1, c_all - 1)
     for c in range(1, c_all):

time: 109 us -> 99.9 us (0.917)
  Pallas kernels: 108 us -> 99.2 us
    pallas_call x1, Pallas kernels: 106 us -> 96.9 us  [local(): pl.pallas_call(functools.partial(kernel, (n, x, f)), out_shape=(jax.Shape...]
where the time goes in v3:
time: 99.9 us; the launch traced here: 99.8 us
  Pallas kernels  99.2 us (99%)
    pallas_call x1, Pallas kernels, local(): pl.pallas_call(functools.partial(kernel, (n, x, f)), out_shape=(jax.Shape...  96.9 us
    pallas_call x1, Pallas kernels, local(): pl.pallas_call(store, out_shape=tuple((jax.ShapeDtypeStruct(result.shape,...  2.31 us

profile of v3, /device:TPU:1, one launch (start us, length us, event | category | flops | bytes accessed | tf_op | source)
XLA Modules:
  0.0 99.8 jit_solution(1977318008977887960)
XLA Ops:
  0.6 96.9 %window.1 = (bf16[512,768]{1,0:T(8,128)(2,1)S(1)}, bf16[64,4,768]{2,1,0:T(4,128)(2,1)S(1)}, bf16[3,512,768]{2,1,0:T(8,128)(2,1)S(1)}, bf16[3,64,4,768]{3,2,1,0:T(4,128)(2,1)S(1)}) custom-call(bf16[3,512,768]{2,1,0:T(8,128)(2,1)} %vq_hbm.1, bf16[3,64,4,768]{3,2,1,0:T(4,128)(2,1)} %aq_hbm.1, f32[2,768]{1,0:T(2,128)} %vg_hbm.1, f32[2,768]{1,0:T(2,128)} %ag_hbm.1, ...), custom_call_target="tpu_custom_call" | custom-call | tf_op jit(solution)/shard_map/window/pallas_call | solution.py:599
  97.5 2.3 %store.1 = (bf16[512,768]{1,0:T(8,128)(2,1)}, bf16[64,4,768]{2,1,0:T(4,128)(2,1)}, bf16[3,512,768]{2,1,0:T(8,128)(2,1)}, bf16[3,64,4,768]{3,2,1,0:T(4,128)(2,1)}) custom-call(bf16[512,768]{1,0:T(8,128)(2,1)S(1)} %get-tuple-element.8.ov, bf16[64,4,768]{2,1,0:T(4,128)(2,1)S(1)} %get-tuple-element.9.oa, bf16[3,512,768]{2,1,0:T(8,128)(2,1)S(1)} %get-tuple-element.10.gv, ...), custom_call_target="tpu_custom_call" | custom-call | tf_op jit(solution)/shard_map/store/pallas_call | solution.py:618

commit v4 on v3

--- a/solution.py
+++ b/solution.py
@@ -405,9 +405,6 @@
                 evs[1, kind, :, at] = sums[kind][5].astype(BF16)
                 for e in range(4):
                     dvkv[kind, e * VBLK : (e + 1) * VBLK, at] = sums[kind][e + 1]
-        for copy in grad_halo(evs, evr, ev_send, ev_recv, c):
-            copy.start()
-
         @pl.when(c > 0)
         def _():
             finish(c - 1)
@@ -441,6 +438,8 @@
                 for e in range(4):
                     dakv[kind, (e + 1) * ga_rows : (e + 2) * ga_rows, at] = sums[kind][e + 1]
         for copy in grad_halo(eas, ear, ea_send, ea_recv, c):
+            copy.start()
+        for copy in grad_halo(evs, evr, ev_send, ev_recv, c):
             copy.start()
 
         @pl.when(c < c_all - 1)

time: 99.9 us -> 104 us (1.041)
  Pallas kernels: 99.2 us -> 103 us
    pallas_call x1, Pallas kernels: 96.9 us -> 101 us  [local(): pl.pallas_call(functools.partial(kernel, (n, x, f)), out_shape=(jax.Shape...]
where the time goes in v4:
time: 104 us
  Pallas kernels  103 us (99%)
    pallas_call x1, Pallas kernels, local(): pl.pallas_call(functools.partial(kernel, (n, x, f)), out_shape=(jax.Shape...  101 us
    pallas_call x1, Pallas kernels, local(): pl.pallas_call(store, out_shape=tuple((jax.ShapeDtypeStruct(result.shape,...  2.31 us

profile of v4, /device:TPU:1, one launch (start us, length us, event | category | flops | bytes accessed | tf_op | source)
XLA Modules:
  0.0 103.7 jit_solution(11168503404091999673)
XLA Ops:
  0.6 100.8 %window.1 = (bf16[512,768]{1,0:T(8,128)(2,1)S(1)}, bf16[64,4,768]{2,1,0:T(4,128)(2,1)S(1)}, bf16[3,512,768]{2,1,0:T(8,128)(2,1)S(1)}, bf16[3,64,4,768]{3,2,1,0:T(4,128)(2,1)S(1)}) custom-call(bf16[3,512,768]{2,1,0:T(8,128)(2,1)} %vq_hbm.1, bf16[3,64,4,768]{3,2,1,0:T(4,128)(2,1)} %aq_hbm.1, f32[2,768]{1,0:T(2,128)} %vg_hbm.1, f32[2,768]{1,0:T(2,128)} %ag_hbm.1, ...), custom_call_target="tpu_custom_call" | custom-call | tf_op jit(solution)/shard_map/window/pallas_call | solution.py:598
  101.4 2.3 %store.1 = (bf16[512,768]{1,0:T(8,128)(2,1)}, bf16[64,4,768]{2,1,0:T(4,128)(2,1)}, bf16[3,512,768]{2,1,0:T(8,128)(2,1)}, bf16[3,64,4,768]{3,2,1,0:T(4,128)(2,1)}) custom-call(bf16[512,768]{1,0:T(8,128)(2,1)S(1)} %get-tuple-element.8.ov, bf16[64,4,768]{2,1,0:T(4,128)(2,1)S(1)} %get-tuple-element.9.oa, bf16[3,512,768]{2,1,0:T(8,128)(2,1)S(1)} %get-tuple-element.10.gv, ...), custom_call_target="tpu_custom_call" | custom-call | tf_op jit(solution)/shard_map/store/pallas_call | solution.py:617
